TPU v7x, 256 devices: a whole 4x4x8 slice. The times are simulated.
256 devices in a mesh: ctx: 16 (over z, core), head: 16 (over x, y).
Axes of the slice: x: 4, y: 4, z: 8, core: 2. Of those that a mesh axis runs over, the one named last changes fastest.
Arguments:
- q_rows: bfloat16 [8192, 2048], P('ctx', 'head'), may hold values from -6 to 6
- k_rows: bfloat16 [8192, 2048], P('ctx', 'head'), may hold values from -6 to 6
- v_rows: bfloat16 [8192, 4096], P('ctx', 'head'), may hold values from -6 to 6
- gate_rows: bfloat16 [8192, 4096], P('ctx', 'head'), may hold values from -6 to 6
- beta_logits: bfloat16 [8192, 32], P('ctx', 'head'), may hold values from -10 to 4
- log_decay: bfloat16 [8192, 32], P('ctx', 'head'), may hold values from -0.7 to 0
- norm_gain: float32 [128], replicated, may hold values from 0.1 to 1.9
- out_weight: bfloat16 [4096, 2048], P('head'), may hold values from -0.09375 to 0.09375
- prompt_blocks: int32 [8], replicated, may hold values from 1 to 32, as said below
- arrival_slot: int32 [64], replicated, may hold values from 0 to 63, as said below
Outputs:
- layer_out: bfloat16 [8192, 2048], P(('ctx', 'head'))
Inputs may be any that keep to these rules, and one draw needn't show every extreme that they name: A permutation; block b arrives at ctx index arrival_slot[b] // 4, and the blocks of ctx index c in stream order are c * 4 to c * 4 + 3. Every ctx index receives at most 2 of its blocks from one ctx index, and exactly 2 from some. `prompt_blocks`: the last prompt has exactly 32 blocks.
All inputs are finite; a program needn't handle non-finite values.
Results may differ from a plain program's by a relative error of at most 0.0049.
Values may be sent and summed in bfloat16 or wider, within the bound.
A program may use at most 128 MiB of HBM per device.

v0:
```python
import jax
import jax.numpy as jnp
from jax import lax
from jax.sharding import PartitionSpec as P

HK = 16
HV = 32
DK = 128
DV = 128
SPAN = 128


def from_behind(shard, axis, by):
    length = lax.axis_size(axis)
    pairs = [(i, i + by) for i in range(length) if 0 <= i + by < length]
    return lax.ppermute(shard, axis, pairs)


def unit_rows(value_rows):
    return value_rows * lax.rsqrt(jnp.sum(value_rows * value_rows, axis=-1, keepdims=True) + 1e-06)


def matrix_product(form, left, right):
    return jnp.einsum(form, left, right, precision=lax.Precision.HIGHEST)


def span_terms(queries, keys_in, value_rows, beta, decay):
    width = queries.shape[0]
    row_ids = jnp.arange(width, dtype=jnp.int32)
    incl = row_ids[:, None] >= row_ids[None, :]
    strict = row_ids[:, None] > row_ids[None, :]
    cumulative = jnp.dot(incl.astype(jnp.float32), decay, precision=lax.Precision.HIGHEST)
    spread = cumulative[:, None] - cumulative[None, :]
    ratio = jnp.where(incl, jnp.exp(jnp.where(incl, spread, 0.0)), 0.0)
    key_key = matrix_product("ik,jk->ij", keys_in, keys_in)
    lower = jnp.where(strict, beta[:, None] * ratio * key_key, 0.0)
    growth = jnp.exp(cumulative)
    rhs = jnp.concatenate([beta[:, None] * value_rows, (beta * growth)[:, None] * keys_in], axis=1)
    solved = jax.scipy.linalg.solve_triangular(
        jnp.eye(width, dtype=jnp.float32) + lower, rhs, lower=True, unit_diagonal=True
    )
    w_value = solved[:, : value_rows.shape[1]]
    w_key = solved[:, value_rows.shape[1] :]
    attend = ratio * matrix_product("ik,jk->ij", queries, keys_in)
    local_output = matrix_product("ij,jv->iv", attend, w_value)
    query_lookup = growth[:, None] * queries - matrix_product("ij,jk->ik", attend, w_key)
    tail = jnp.exp(cumulative[-1] - cumulative)[:, None] * keys_in
    transit = jnp.exp(cumulative[-1]) * jnp.eye(
        keys_in.shape[1], dtype=jnp.float32
    ) - matrix_product("jk,jl->kl", tail, w_key)
    offset = matrix_product("jk,jv->kv", tail, w_value)
    return (query_lookup, local_output, transit, offset)


def per_device(
    q_rows,
    k_rows,
    v_rows,
    gate_rows,
    beta_logits,
    log_decay,
    norm_gain,
    out_weight,
    prompt_blocks,
    arrival_slot,
):
    peers = lax.axis_size("ctx")
    myself = lax.axis_index("ctx")
    tokens_here = q_rows.shape[0]
    block_count = tokens_here // SPAN
    total_blocks = block_count * peers
    capacity = max(2, block_count // peers + 1)
    stream_ids = jnp.arange(total_blocks, dtype=jnp.int32)
    sources = arrival_slot // block_count
    targets = stream_ids // block_count
    paired = (
        (sources[:, None] == sources[None, :])
        & (targets[:, None] == targets[None, :])
        & (stream_ids[None, :] < stream_ids[:, None])
    )
    rank_pair = jnp.sum(paired.astype(jnp.int32), axis=1)
    send_slot = targets * capacity + rank_pair
    recv_slot = sources * capacity + rank_pair
    local_ids = jnp.arange(block_count, dtype=jnp.int32)
    mine_arrived = arrival_slot[None, :] == (myself * block_count + local_ids)[:, None]
    send_key = jnp.sum(jnp.where(mine_arrived, send_slot[None, :], 0), axis=1)
    positions = jnp.arange(peers * capacity, dtype=jnp.int32)
    send_from = jnp.sum(
        jnp.where(send_key[None, :] == positions[:, None], local_ids[None, :], 0), axis=1
    )
    recv_key = lax.dynamic_slice_in_dim(recv_slot, myself * block_count, block_count)
    back_from = jnp.sum(
        jnp.where(recv_key[None, :] == positions[:, None], local_ids[None, :], 0), axis=1
    )
    plan_ids = myself * block_count + local_ids
    starts = jnp.cumsum(prompt_blocks) - prompt_blocks
    keep = jnp.where(jnp.any(plan_ids[:, None] == starts[None, :], axis=1), 0.0, 1.0).astype(
        jnp.float32
    )

    def to_buffer(rows):
        return jnp.take(rows.reshape(block_count, SPAN, -1), send_from, axis=0)

    sent = (
        lax.all_to_all(to_buffer(q_rows), "ctx", split_axis=0, concat_axis=0, tiled=True),
        lax.all_to_all(to_buffer(k_rows), "ctx", split_axis=0, concat_axis=0, tiled=True),
        lax.all_to_all(to_buffer(v_rows), "ctx", split_axis=0, concat_axis=0, tiled=True),
        lax.all_to_all(to_buffer(gate_rows), "ctx", split_axis=0, concat_axis=0, tiled=True),
        lax.all_to_all(to_buffer(beta_logits), "ctx", split_axis=0, concat_axis=0, tiled=True),
        lax.all_to_all(to_buffer(log_decay), "ctx", split_axis=0, concat_axis=0, tiled=True),
    )
    q_plan, k_plan, v_plan, g_plan, b_plan, d_plan = [
        jnp.take(piece, recv_key, axis=0) for piece in sent
    ]
    heads_here = v_plan.shape[2] // DV
    key_heads = q_plan.shape[2] // DK
    ratio_heads = HV // HK
    queries = unit_rows(
        q_plan.astype(jnp.float32).reshape(block_count, SPAN, key_heads, DK)
    ) * DK ** (-0.5)
    keys_all = unit_rows(k_plan.astype(jnp.float32).reshape(block_count, SPAN, key_heads, DK))
    queries = jnp.repeat(queries, ratio_heads, axis=2)
    keys_all = jnp.repeat(keys_all, ratio_heads, axis=2)
    value_rows = v_plan.astype(jnp.float32).reshape(block_count, SPAN, heads_here, DV)
    beta = jax.nn.sigmoid(b_plan.astype(jnp.float32))
    decay = d_plan.astype(jnp.float32)
    batched = jax.vmap(jax.vmap(span_terms, in_axes=(1, 1, 1, 1, 1)))
    query_lookup, local_output, transit, offset = batched(
        queries, keys_all, value_rows, beta, decay
    )
    identity = jnp.broadcast_to(jnp.eye(DK, dtype=jnp.float32), (heads_here, DK, DK))
    empty = jnp.zeros((heads_here, DK, DV), jnp.float32)

    def compose(carry, inputs):
        linear, shifted = carry
        transit_b, offset_b, keep_b = inputs
        linear = keep_b * linear
        shifted = keep_b * shifted
        return (
            (
                matrix_product("hij,hjk->hik", transit_b, linear),
                matrix_product("hij,hjv->hiv", transit_b, shifted) + offset_b,
            ),
            None,
        )

    (segment_map, segment_shift), _ = lax.scan(compose, (identity, empty), (transit, offset, keep))

    def relay(step_index, state_in):
        outgoing = matrix_product("hij,hjv->hiv", segment_map, state_in) + segment_shift
        return from_behind(outgoing, "ctx", 1)

    entry_state = lax.fori_loop(0, peers - 1, relay, empty)

    def emit(running_state, inputs):
        query_block, local_block, transit_b, offset_b, keep_b = inputs
        running_state = keep_b * running_state
        delta_kernel = matrix_product("egu,euq->egq", query_block, running_state) + local_block
        return (matrix_product("hij,hjv->hiv", transit_b, running_state) + offset_b, delta_kernel)

    _, cores = lax.scan(emit, entry_state, (query_lookup, local_output, transit, offset, keep))
    cores = jnp.transpose(cores, (0, 2, 1, 3))
    gates = g_plan.astype(jnp.float32).reshape(block_count, SPAN, heads_here, DV)
    scale = lax.rsqrt(jnp.mean(cores * cores, axis=-1, keepdims=True) + 1e-06)
    normed = (cores * scale * norm_gain * jax.nn.silu(gates)).astype(jnp.bfloat16)
    normed = normed.reshape(block_count, SPAN, heads_here * DV)
    returned = lax.all_to_all(
        jnp.take(normed, back_from, axis=0), "ctx", split_axis=0, concat_axis=0, tiled=True
    )
    arrived = jnp.take(returned, send_key, axis=0).reshape(tokens_here, heads_here * DV)
    finished = lax.psum_scatter(
        jnp.dot(arrived, out_weight, preferred_element_type=jnp.float32),
        "head",
        scatter_dimension=0,
        tiled=True,
    )
    return finished.astype(jnp.bfloat16)


def solution(mesh):
    in_specs = (
        P("ctx", "head"),
        P("ctx", "head"),
        P("ctx", "head"),
        P("ctx", "head"),
        P("ctx", "head"),
        P("ctx", "head"),
        P(),
        P("head", None),
        P(),
        P(),
    )
    out_specs = P(("ctx", "head"), None)
    return jax.shard_map(
        per_device, mesh=mesh, in_specs=in_specs, out_specs=out_specs, check_vma=False
    )
```

profile of v0, /device:TPU:1, one launch (start us, length us, event | category | flops | bytes accessed | tf_op | source)
XLA Modules:
  0.0 566.9 jit_solution(7619160209144087535)
XLA Ops:
  11.5 10.0 %all-to-all-start = ((bf16[32,128,2]{1,2,0:T(2,128)(2,1)}), bf16[32,128,2]{1,2,0:T(2,128)(2,1)S(1)}, u32[]{:S(2)}, u32[]{:S(2)}) async-start(bf16[32,128,2]{1,2,0:T(2,128)(2,1)} %get-tuple-element.186), calls=%async_computation | async-start | bytes 32768 | tf_op jit(solution)/shard_map/all_to_all | solution.py:110
  23.0 5.8 %all-to-all-done = bf16[32,128,2]{1,2,0:T(2,128)(2,1)S(1)} async-done(((bf16[32,128,2]{1,2,0:T(2,128)(2,1)}), bf16[32,128,2]{1,2,0:T(2,128)(2,1)S(1)}, u32[]{:S(2)}, u32[]{:S(2)}) %all-to-all-start) | async-done | bytes 16416 | tf_op jit(solution)/shard_map/all_to_all | solution.py:110
  28.8 3.7 all-to-all-start.2
  34.1 5.8 %all-to-all-done.2 = bf16[32,128,2]{1,2,0:T(2,128)(2,1)S(1)} async-done(((bf16[32,128,2]{1,2,0:T(2,128)(2,1)}), bf16[32,128,2]{1,2,0:T(2,128)(2,1)S(1)}, u32[]{:S(2)}, u32[]{:S(2)}) %all-to-all-start.2) | async-done | bytes 16416 | tf_op jit(solution)/shard_map/all_to_all | solution.py:109
  39.9 33.3 %all_to_all.35 = bf16[32,128,128]{2,1,0:T(8,128)(2,1)} all-to-all(bf16[32,128,128]{2,1,0:T(8,128)(2,1)} %get-tuple-element.183), channel_id=1, replica_groups=mesh['ctx'=16,'head'=16] {'ctx'}, dimensions={0} | all-to-all | bytes 2097152 | tf_op jit(solution)/shard_map/all_to_all | solution.py:106
  73.2 3.6 all-to-all-start.4
  76.8 2.0 gather_fusion.6
  78.8 2.0 gather_fusion.10
  80.8 4.6 broadcast_select_fusion.1
  85.5 18.6 %all-to-all-done.4 = bf16[32,128,128]{2,1,0:T(8,128)(2,1)S(1)} async-done(((bf16[32,128,128]{2,1,0:T(8,128)(2,1)}), bf16[32,128,128]{2,1,0:T(8,128)(2,1)S(1)}, u32[]{:S(2)}, u32[]{:S(2)}) %all-to-all-start.4) | async-done | bytes 1048608 | tf_op jit(solution)/shard_map/all_to_all | solution.py:105
  105.1 3.6 all-to-all-start.3
  109.1 48.5 %all-to-all-done.3 = bf16[32,128,256]{2,1,0:T(8,128)(2,1)S(1)} async-done(((bf16[32,128,256]{2,1,0:T(8,128)(2,1)}), bf16[32,128,256]{2,1,0:T(8,128)(2,1)S(1)}, u32[]{:S(2)}, u32[]{:S(2)}) %all-to-all-start.3) | async-done | bytes 2097184 | tf_op jit(solution)/shard_map/all_to_all | solution.py:107
  158.9 5.0 all-to-all-start.5
  173.7 79.2 %custom-call.4 = f32[4,2,1,128,128]{3,4,2,1,0:T(8,128)} custom-call(f32[4,2,1,128,128]{4,3,2,1,0:T(8,128)S(1)} %fusion.28), custom_call_target="InvertDiagBlocksLowerTriangular" | custom-call | tf_op jit(solution)/shard_map/vmap(vmap(jit(_solve_triangular)))/triangular_solve | solution.py:39
  254.3 2.2 gather_fusion.7
  256.5 2.9 gather_fusion.11
  263.7 2.1 fusion.29
  270.3 9.9 %while.37 = (s32[]{:T(128)}, f32[2,128,128]{2,1,0:T(8,128)S(1)}, f32[2,128,128]{2,1,0:T(8,128)S(1)}, f32[4,2,128,128]{3,2,1,0:T(8,128)S(1)}, f32[4]{0:T(128)S(1)...) while((s32[]{:T(128)}, f32[2,128,128]{2,1,0:T(8,128)S(1)}, ...), condition=%wide.region_7.14_spmd.clone, body=%wide.region_6.13_spmd.clone.sunk | while | flops 100794368 | bytes 1443443 | solution.py:147
  280.3 97.6 %while.35 = (s32[]{:T(128)}, f32[2,128,128]{2,1,0:T(8,128)S(1)}, f32[2,128,128]{2,1,0:T(8,128)S(1)}, f32[2,128,128]{2,1,0:T(8,128)S(1)}, s32[]{:T(128)}) while((s32[]{:T(128)}, f32[2,128,128]{2,1,0:T(8,128)S(1)}, f32[2,128,128]{2,1,0:T(8,128)S(1)}, f32[2,128,128]{2,1,0:T(8,128)S(1)}, s32[]{:T(128)}) %tuple.70), condition=%wide.region_9.16_spmd, body=%wide.region_8.15_spmd.sunk | while | flops 50364416 | bytes 1048677 | solution.py:153
  280.6 3.5 collective-permute-start
  284.1 1.9 collective-permute-done
  286.3 4.4 collective-permute-start
  290.7 1.9 collective-permute-done
  292.9 4.4 collective-permute-start
  297.2 1.9 collective-permute-done
  299.4 4.4 collective-permute-start
  303.8 1.9 collective-permute-done
  306.0 4.4 collective-permute-start
  310.4 1.9 collective-permute-done
  312.6 4.4 collective-permute-start
  316.9 1.9 collective-permute-done
  319.1 4.4 collective-permute-start
  325.7 4.4 collective-permute-start
  332.2 4.4 collective-permute-start
  336.6 1.9 collective-permute-done
  338.8 4.4 collective-permute-start
  345.4 4.4 collective-permute-start
  351.9 4.4 collective-permute-start
  356.3 1.9 collective-permute-done
  358.5 4.4 collective-permute-start
  365.0 4.4 collective-permute-start
  371.6 4.4 collective-permute-start
  376.0 1.9 collective-permute-done
  377.9 16.5 %while.36 = (s32[]{:T(128)}, f32[2,128,128]{2,1,0:T(8,128)S(1)}, f32[4,2,128,128]{2,3,1,0:T(8,128)}, f32[4,2,128,128]{3,2,1,0:T(8,128)S(1)}, f32[4]{0:T(128)S(1)...) while((s32[]{:T(128)}, f32[2,128,128]{2,1,0:T(8,128)S(1)}, ...), condition=%wide.region_12.19_spmd, body=%wide.region_11.18_spmd.sunk | while | flops 100794368 | bytes 1838697 | solution.py:161
  399.7 26.3 %all-to-all-start.6 = ((bf16[32,128,256]{1,2,0:T(8,128)(2,1)}), bf16[32,128,256]{1,2,0:T(8,128)(2,1)S(1)}, u32[]{:S(2)}, u32[]{:S(2)}) async-start(bf16[32,128,256]{1,2,0:T(8,128)(2,1)} %broadcast_select_fusion), calls=%async_computation.6 | async-start | bytes 4194304 | tf_op jit(solution)/shard_map/all_to_all | solution.py:167
  426.1 48.9 %all-to-all-done.6 = bf16[32,128,256]{1,2,0:T(8,128)(2,1)S(1)} async-done(((bf16[32,128,256]{1,2,0:T(8,128)(2,1)}), bf16[32,128,256]{1,2,0:T(8,128)(2,1)S(1)}, u32[]{:S(2)}, u32[]{:S(2)}) %all-to-all-start.6) | async-done | bytes 2097184 | tf_op jit(solution)/shard_map/all_to_all | solution.py:167
  475.8 2.7 fusion.65
  478.5 79.9 %reduce-scatter.2.cloned.1.call-done = f32[32,2048]{1,0:T(8,128)} async-done(((f32[512,2048]{1,0:T(8,128)}), f32[32,2048]{1,0:T(8,128)}) %reduce-scatter.2.cloned.1.call-update) | async-done | bytes 262160 | tf_op jit(solution)/shard_map/reduce_scatter | solution.py:171
  (182 shorter events, 79.9 us)
Async XLA Ops:
  6.5 469.3 %copy-start = (bf16[256,2048]{1,0:T(8,128)(2,1)S(1)}, bf16[256,2048]{1,0:T(8,128)(2,1)}, u32[]{:S(2)}) copy-start(bf16[256,2048]{1,0:T(8,128)(2,1)} %param.35) | copy-start | bytes 3145732
  6.5 3.6 copy-start.1
  8.4 0.5 copy-start.14
  8.9 12.6 %copy-start.4 = (bf16[512,128]{1,0:T(8,128)(2,1)S(1)}, bf16[512,128]{1,0:T(8,128)(2,1)}, u32[]{:S(2)}) copy-start(bf16[512,128]{1,0:T(8,128)(2,1)} %param.29) | copy-start | bytes 393220
  10.2 12.1 %copy-start.5 = (bf16[512,128]{1,0:T(8,128)(2,1)S(1)}, bf16[512,128]{1,0:T(8,128)(2,1)}, u32[]{:S(2)}) copy-start(bf16[512,128]{1,0:T(8,128)(2,1)} %param.28) | copy-start | bytes 393220
  11.5 17.3 %all-to-all-start = ((bf16[32,128,2]{1,2,0:T(2,128)(2,1)}), bf16[32,128,2]{1,2,0:T(2,128)(2,1)S(1)}, u32[]{:S(2)}, u32[]{:S(2)}) async-start(bf16[32,128,2]{1,2,0:T(2,128)(2,1)} %get-tuple-element.186), calls=%async_computation | async-start | bytes 32768 | tf_op jit(solution)/shard_map/all_to_all | solution.py:110
  28.8 11.1 %all-to-all-start.2 = ((bf16[32,128,2]{1,2,0:T(2,128)(2,1)}), bf16[32,128,2]{1,2,0:T(2,128)(2,1)S(1)}, u32[]{:S(2)}, u32[]{:S(2)}) async-start(bf16[32,128,2]{1,2,0:T(2,128)(2,1)} %get-tuple-element.185), calls=%async_computation.2 | async-start | bytes 32768 | tf_op jit(solution)/shard_map/all_to_all | solution.py:109
  39.9 36.8 %copy-start.2 = (bf16[512,256]{1,0:T(8,128)(2,1)S(1)}, bf16[512,256]{1,0:T(8,128)(2,1)}, u32[]{:S(2)}) copy-start(bf16[512,256]{1,0:T(8,128)(2,1)} %param.30) | copy-start | bytes 786436
  73.2 30.9 %all-to-all-start.4 = ((bf16[32,128,128]{2,1,0:T(8,128)(2,1)}), bf16[32,128,128]{2,1,0:T(8,128)(2,1)S(1)}, u32[]{:S(2)}, u32[]{:S(2)}) async-start(bf16[32,128,128]{2,1,0:T(8,128)(2,1)} %get-tuple-element.184), calls=%async_computation.4 | async-start | bytes 2097152 | tf_op jit(solution)/shard_map/all_to_all | solution.py:105
  76.8 2.0 copy-start.3
  104.0 1.0 copy-start.8
  104.0 4.7 copy-start.16
  105.1 52.5 %all-to-all-start.3 = ((bf16[32,128,256]{2,1,0:T(8,128)(2,1)}), bf16[32,128,256]{2,1,0:T(8,128)(2,1)S(1)}, u32[]{:S(2)}, u32[]{:S(2)}) async-start(bf16[32,128,256]{2,1,0:T(8,128)(2,1)} %get-tuple-element.180), calls=%async_computation.3 | async-start | bytes 4194304 | tf_op jit(solution)/shard_map/all_to_all | solution.py:107
  157.6 1.3 copy-start.6
  158.9 97.6 %all-to-all-start.5 = ((bf16[32,128,256]{2,1,0:T(8,128)(2,1)}), bf16[32,128,256]{2,1,0:T(8,128)(2,1)}, u32[]{:S(2)}, u32[]{:S(2)}) async-start(bf16[32,128,256]{2,1,0:T(8,128)(2,1)} %get-tuple-element.179), calls=%async_computation.5 | async-start | bytes 4194304 | tf_op jit(solution)/shard_map/all_to_all | solution.py:108
  164.7 9.0 %copy-start.9 = (f32[128,128]{1,0:T(8,128)}, f32[128,128]{1,0:T(8,128)S(1)}, u32[]{:S(2)}) copy-start(f32[128,128]{1,0:T(8,128)S(1)} %get-tuple-element.193) | copy-start | bytes 196612
  265.8 3.3 copy-start.10
  265.8 3.3 copy-start.11
  266.5 3.9 copy-start.17
  280.6 5.5 collective-permute-start
  286.3 6.3 %collective-permute-start = (f32[2,128,128]{2,1,0:T(8,128)S(1)}, f32[2,128,128]{2,1,0:T(8,128)S(1)}, u32[]{:S(2)}, u32[]{:S(2)}) collective-permute-start(f32[2,128,128]{2,1,0:T(8,128)S(1)} %convolution_add_fusion.7), channel_id=1, source_target_pairs={{0,16},{16,32},{32,48},{48,64},{64,80},{80,96},{96,112},{112,128},... | collective-permute-start | bytes 393224 | tf_op jit(solution)/shard_map/while/body/eval_jaxpr/ppermute | solution.py:16
  292.9 6.3 %collective-permute-start = (f32[2,128,128]{2,1,0:T(8,128)S(1)}, f32[2,128,128]{2,1,0:T(8,128)S(1)}, u32[]{:S(2)}, u32[]{:S(2)}) collective-permute-start(f32[2,128,128]{2,1,0:T(8,128)S(1)} %convolution_add_fusion.7), channel_id=1, source_target_pairs={{0,16},{16,32},{32,48},{48,64},{64,80},{80,96},{96,112},{112,128},... | collective-permute-start | bytes 393224 | tf_op jit(solution)/shard_map/while/body/eval_jaxpr/ppermute | solution.py:16
  299.4 6.3 %collective-permute-start = (f32[2,128,128]{2,1,0:T(8,128)S(1)}, f32[2,128,128]{2,1,0:T(8,128)S(1)}, u32[]{:S(2)}, u32[]{:S(2)}) collective-permute-start(f32[2,128,128]{2,1,0:T(8,128)S(1)} %convolution_add_fusion.7), channel_id=1, source_target_pairs={{0,16},{16,32},{32,48},{48,64},{64,80},{80,96},{96,112},{112,128},... | collective-permute-start | bytes 393224 | tf_op jit(solution)/shard_map/while/body/eval_jaxpr/ppermute | solution.py:16
  306.0 6.3 %collective-permute-start = (f32[2,128,128]{2,1,0:T(8,128)S(1)}, f32[2,128,128]{2,1,0:T(8,128)S(1)}, u32[]{:S(2)}, u32[]{:S(2)}) collective-permute-start(f32[2,128,128]{2,1,0:T(8,128)S(1)} %convolution_add_fusion.7), channel_id=1, source_target_pairs={{0,16},{16,32},{32,48},{48,64},{64,80},{80,96},{96,112},{112,128},... | collective-permute-start | bytes 393224 | tf_op jit(solution)/shard_map/while/body/eval_jaxpr/ppermute | solution.py:16
  312.6 6.3 %collective-permute-start = (f32[2,128,128]{2,1,0:T(8,128)S(1)}, f32[2,128,128]{2,1,0:T(8,128)S(1)}, u32[]{:S(2)}, u32[]{:S(2)}) collective-permute-start(f32[2,128,128]{2,1,0:T(8,128)S(1)} %convolution_add_fusion.7), channel_id=1, source_target_pairs={{0,16},{16,32},{32,48},{48,64},{64,80},{80,96},{96,112},{112,128},... | collective-permute-start | bytes 393224 | tf_op jit(solution)/shard_map/while/body/eval_jaxpr/ppermute | solution.py:16
  319.1 6.3 %collective-permute-start = (f32[2,128,128]{2,1,0:T(8,128)S(1)}, f32[2,128,128]{2,1,0:T(8,128)S(1)}, u32[]{:S(2)}, u32[]{:S(2)}) collective-permute-start(f32[2,128,128]{2,1,0:T(8,128)S(1)} %convolution_add_fusion.7), channel_id=1, source_target_pairs={{0,16},{16,32},{32,48},{48,64},{64,80},{80,96},{96,112},{112,128},... | collective-permute-start | bytes 393224 | tf_op jit(solution)/shard_map/while/body/eval_jaxpr/ppermute | solution.py:16
  325.7 6.3 %collective-permute-start = (f32[2,128,128]{2,1,0:T(8,128)S(1)}, f32[2,128,128]{2,1,0:T(8,128)S(1)}, u32[]{:S(2)}, u32[]{:S(2)}) collective-permute-start(f32[2,128,128]{2,1,0:T(8,128)S(1)} %convolution_add_fusion.7), channel_id=1, source_target_pairs={{0,16},{16,32},{32,48},{48,64},{64,80},{80,96},{96,112},{112,128},... | collective-permute-start | bytes 393224 | tf_op jit(solution)/shard_map/while/body/eval_jaxpr/ppermute | solution.py:16
  332.2 6.3 %collective-permute-start = (f32[2,128,128]{2,1,0:T(8,128)S(1)}, f32[2,128,128]{2,1,0:T(8,128)S(1)}, u32[]{:S(2)}, u32[]{:S(2)}) collective-permute-start(f32[2,128,128]{2,1,0:T(8,128)S(1)} %convolution_add_fusion.7), channel_id=1, source_target_pairs={{0,16},{16,32},{32,48},{48,64},{64,80},{80,96},{96,112},{112,128},... | collective-permute-start | bytes 393224 | tf_op jit(solution)/shard_map/while/body/eval_jaxpr/ppermute | solution.py:16
  338.8 6.3 %collective-permute-start = (f32[2,128,128]{2,1,0:T(8,128)S(1)}, f32[2,128,128]{2,1,0:T(8,128)S(1)}, u32[]{:S(2)}, u32[]{:S(2)}) collective-permute-start(f32[2,128,128]{2,1,0:T(8,128)S(1)} %convolution_add_fusion.7), channel_id=1, source_target_pairs={{0,16},{16,32},{32,48},{48,64},{64,80},{80,96},{96,112},{112,128},... | collective-permute-start | bytes 393224 | tf_op jit(solution)/shard_map/while/body/eval_jaxpr/ppermute | solution.py:16
  345.4 6.3 %collective-permute-start = (f32[2,128,128]{2,1,0:T(8,128)S(1)}, f32[2,128,128]{2,1,0:T(8,128)S(1)}, u32[]{:S(2)}, u32[]{:S(2)}) collective-permute-start(f32[2,128,128]{2,1,0:T(8,128)S(1)} %convolution_add_fusion.7), channel_id=1, source_target_pairs={{0,16},{16,32},{32,48},{48,64},{64,80},{80,96},{96,112},{112,128},... | collective-permute-start | bytes 393224 | tf_op jit(solution)/shard_map/while/body/eval_jaxpr/ppermute | solution.py:16
  351.9 6.3 %collective-permute-start = (f32[2,128,128]{2,1,0:T(8,128)S(1)}, f32[2,128,128]{2,1,0:T(8,128)S(1)}, u32[]{:S(2)}, u32[]{:S(2)}) collective-permute-start(f32[2,128,128]{2,1,0:T(8,128)S(1)} %convolution_add_fusion.7), channel_id=1, source_target_pairs={{0,16},{16,32},{32,48},{48,64},{64,80},{80,96},{96,112},{112,128},... | collective-permute-start | bytes 393224 | tf_op jit(solution)/shard_map/while/body/eval_jaxpr/ppermute | solution.py:16
  358.5 6.3 %collective-permute-start = (f32[2,128,128]{2,1,0:T(8,128)S(1)}, f32[2,128,128]{2,1,0:T(8,128)S(1)}, u32[]{:S(2)}, u32[]{:S(2)}) collective-permute-start(f32[2,128,128]{2,1,0:T(8,128)S(1)} %convolution_add_fusion.7), channel_id=1, source_target_pairs={{0,16},{16,32},{32,48},{48,64},{64,80},{80,96},{96,112},{112,128},... | collective-permute-start | bytes 393224 | tf_op jit(solution)/shard_map/while/body/eval_jaxpr/ppermute | solution.py:16
  365.0 6.3 %collective-permute-start = (f32[2,128,128]{2,1,0:T(8,128)S(1)}, f32[2,128,128]{2,1,0:T(8,128)S(1)}, u32[]{:S(2)}, u32[]{:S(2)}) collective-permute-start(f32[2,128,128]{2,1,0:T(8,128)S(1)} %convolution_add_fusion.7), channel_id=1, source_target_pairs={{0,16},{16,32},{32,48},{48,64},{64,80},{80,96},{96,112},{112,128},... | collective-permute-start | bytes 393224 | tf_op jit(solution)/shard_map/while/body/eval_jaxpr/ppermute | solution.py:16
  371.6 6.3 %collective-permute-start = (f32[2,128,128]{2,1,0:T(8,128)S(1)}, f32[2,128,128]{2,1,0:T(8,128)S(1)}, u32[]{:S(2)}, u32[]{:S(2)}) collective-permute-start(f32[2,128,128]{2,1,0:T(8,128)S(1)} %convolution_add_fusion.7), channel_id=1, source_target_pairs={{0,16},{16,32},{32,48},{48,64},{64,80},{80,96},{96,112},{112,128},... | collective-permute-start | bytes 393224 | tf_op jit(solution)/shard_map/while/body/eval_jaxpr/ppermute | solution.py:16
  377.9 17.6 %copy-start.7 = (f32[4,128,256]{2,1,0:T(8,128)S(1)}, f32[4,128,256]{2,1,0:T(8,128)}, u32[]{:S(2)}) copy-start(f32[4,128,256]{2,1,0:T(8,128)} %get-tuple-element.177) | copy-start | bytes 1572868
  377.9 17.8 %copy-start.12 = (f32[128]{0:T(128)S(1)}, f32[128]{0:T(128)}, u32[]{:S(2)}) copy-start(f32[128]{0:T(128)} %param.34) | copy-start | bytes 1540
  397.0 1.1 copy-start.13
  399.7 26.4 %copy-start.15 = (s32[4]{0:T(128)S(1)}, s32[4]{0:T(128)}, u32[]{:S(2)}) copy-start(s32[4]{0:T(128)} %copy-done.14) | copy-start | bytes 52
  399.7 75.3 %all-to-all-start.6 = ((bf16[32,128,256]{1,2,0:T(8,128)(2,1)}), bf16[32,128,256]{1,2,0:T(8,128)(2,1)S(1)}, u32[]{:S(2)}, u32[]{:S(2)}) async-start(bf16[32,128,256]{1,2,0:T(8,128)(2,1)} %broadcast_select_fusion), calls=%async_computation.6 | async-start | bytes 4194304 | tf_op jit(solution)/shard_map/all_to_all | solution.py:167
  426.0 132.5 %reduce-scatter.2.cloned.1.call-start = ((), (), s32[]{:S(2)}) async-start(), calls=%async_computation.8 | async-start | bytes 4456448 | tf_op jit(solution)/shard_map/reduce_scatter | solution.py:171
Sparse Core Ops, SparseCore 0:
  478.6 79.7 reduce-scatter.1
where the time goes:
time: 569 us; the launch traced here: 567 us
  waiting for transfers between devices  236 us (41%)
  starting transfers between devices  117 us (21%)
  other arithmetic  99.1 us (17%)
  matrix products  34 us (6%)
  blocking collectives  33.3 us (6%)
  local copies, waits for them, and re-layouts  32.9 us (6%)
  between operations  13.9 us (2%)
    reduce_scatter x1, waiting for transfers between devices, per_device(): lax.psum_scatter(jnp.dot(arrived, out_weight, preferred_element_type=jnp....  79.9 us
    another operation x2, other arithmetic, span_terms(): jax.scipy.linalg.solve_triangular(jnp.eye(width, dtype=jnp.float32) + low...  79.3 us
    ppermute x15, starting transfers between devices, from_behind(): return lax.ppermute(shard, axis, pairs)  64.5 us
    all_to_all x1, waiting for transfers between devices, per_device(): lax.all_to_all(jnp.take(normed, back_from, axis=0), 'ctx', split_axis=0,...  48.9 us
    all_to_all x1, waiting for transfers between devices, per_device(): lax.all_to_all(to_buffer(v_rows), 'ctx', split_axis=0, concat_axis=0, til...  48.5 us
    all_to_all x1, blocking collectives, per_device(): lax.all_to_all(to_buffer(k_rows), 'ctx', split_axis=0, concat_axis=0, til...  33.3 us
    dot_general x37, matrix products, matrix_product(): return jnp.einsum(form, left, right, precision=lax.Precision.HIGHEST)  29.1 us
    ppermute x15, waiting for transfers between devices, from_behind(): return lax.ppermute(shard, axis, pairs)  28.8 us
  transfers between devices with their start and end apart: 22, of which 21 were waited for; matrix products, arithmetic and copies ran while one was open for 18% of the time, Pallas kernels for 0%

commit v1 on v0

v1 whole, which is shorter than its diff:
```python
import jax
import jax.numpy as jnp
from jax import lax
from jax.experimental import pallas as pl
from jax.experimental.pallas import tpu as pltpu
from jax.sharding import PartitionSpec as P

SPAN = 128
DK = 128
DV = 128
HEADS = 2
LOCAL = 4
PEERS = 16
CHIPS = 8
SLICE = 16
BLOCKS = 64
CHAIN = 32
SIDE = 4
MODEL = 2048
PIECES = 4
PIECE = MODEL // PIECES
GROUP = 2
VMEM_LIMIT = 60 * 2**20
MESH = pl.DeviceIdType.MESH
F32 = jnp.float32
BF16 = jnp.bfloat16


def split(x):
    high = x.astype(BF16)
    return high, (x - high.astype(F32)).astype(BF16)


def mm(a, b):
    return jnp.dot(a, b, preferred_element_type=F32)


def mm_t(a, b):
    return lax.dot_general(a, b, (((1,), (1,)), ((), ())), preferred_element_type=F32)


def product(a, b):
    a_high, a_low = a
    b_high, b_low = b
    n = b_high.shape[1]
    if n == 128:
        left = jnp.concatenate([a_high, a_low], axis=1)
        right = jnp.concatenate(
            [
                jnp.concatenate([b_high, b_low], axis=1),
                jnp.concatenate([b_high, jnp.zeros_like(b_low)], axis=1),
            ],
            axis=0,
        )
        both = mm(left, right)
        return both[:, :n] + both[:, n:]
    left = jnp.concatenate([a_high, a_low], axis=1)
    right = jnp.concatenate([b_high, b_high], axis=0)
    return mm(left, right) + mm(a_high, b_low)


def spread_lanes(column):
    return jnp.broadcast_to(column, (column.shape[0], 128))


def block_terms(i, h, q, k, beta_row, decay_row, v, shared, consts):
    tri, strict, incl = consts
    qn, kf, kt2, rk_wide, kk, qk = shared
    beta = jnp.broadcast_to(1.0 / (1.0 + jnp.exp(-beta_row)), (SPAN, SPAN)).T
    steps = jnp.broadcast_to(decay_row, (SPAN, SPAN)).astype(BF16)
    wide = mm_t(tri, steps)
    wide_row = mm_t(steps, tri)
    ratio = jnp.exp(jnp.minimum(wide - wide_row, 0.0))
    lower = jnp.where(strict, beta * ratio * kk, 0.0)
    attend = jnp.where(incl, ratio * qk, 0.0)
    growth = jnp.exp(wide)
    end = wide[SPAN - 1 : SPAN, :]
    tail = jnp.exp(end - wide) * rk_wide
    rhs = jnp.concatenate([beta * v, beta * growth * rk_wide * kf], axis=1)
    return dict(i=i, h=h, lower=lower, attend=attend, tail=tail, rhs=rhs, kt2=kt2, grown=growth * qn, decay=jnp.exp(end))


def main_kernel(
    arr_ref, prompt_ref, q_hbm, k_hbm, v_hbm, gate_hbm, beta_hbm, decay_hbm, gain_hbm, w_ref,
    out_ref,
    q_ref, k_ref, v_ref, gate_ref, beta_ref, decay_ref, gain_ref,
    m_ref, o_ref, d_ref, ql_ref, lo_ref, inv_vmem, inv_ref,
    m_all, o_all, d_all, stream, states, entry, normed, rows_all, w_all, part, got,
    in_sem, inv_sem, w_send, w_recv, w_local, c_send, c_recv, m_send, m_recv, o_send, o_recv, d_send, d_recv,
    s_send, s_recv, n_send, n_recv, p_send, p_recv,
):
    ctx = lax.axis_index("ctx")
    head = lax.axis_index("head")
    chip, core = lax.div(ctx, 2), lax.rem(ctx, 2)
    sibling = 2 * chip + 1 - core
    side_x, side_y = lax.div(head, SIDE), lax.rem(head, SIDE)

    def ctx_peer(k):
        return lax.rem(ctx + k, PEERS)

    def y_peer(k):
        return side_x * SIDE + lax.rem(side_y + k, SIDE)

    def x_peer(k):
        return lax.rem(side_x + k, SIDE) * SIDE + side_y

    barrier = pltpu.get_barrier_semaphore()

    def greet(k, carry):
        pl.semaphore_signal(barrier, inc=1, device_id=(ctx_peer(k), head), device_id_type=MESH)
        return carry

    loads = [
        pltpu.make_async_copy(src, dst, in_sem.at[n])
        for n, (src, dst) in enumerate(
            (
                (k_hbm, k_ref), (q_hbm, q_ref), (beta_hbm, beta_ref), (decay_hbm, decay_ref),
                (v_hbm, v_ref), (gate_hbm, gate_ref), (gain_hbm, gain_ref),
            )
        )
    ]
    for load in loads:
        load.start()
    lax.fori_loop(1, PEERS, greet, 0)
    for k in range(1, SIDE):
        pl.semaphore_signal(barrier, inc=1, device_id=(ctx, y_peer(k)), device_id_type=MESH)
        pl.semaphore_signal(barrier, inc=1, device_id=(ctx, x_peer(k)), device_id_type=MESH)

    def remote(src, dst, send, recv, target):
        return pltpu.make_async_remote_copy(
            src_ref=src, dst_ref=dst, send_sem=send, recv_sem=recv, device_id=target, device_id_type=MESH
        )

    def o_copy(k):
        to = ctx_peer(k)
        return remote(
            o_ref.at[lax.rem(to, 2), lax.div(to, 2)], o_all.at[pl.ds(LOCAL * ctx, LOCAL)],
            o_send.at[k], o_recv.at[k], (to, head),
        )

    def d_copy(k):
        return remote(
            d_ref, d_all.at[pl.ds(pl.multiple_of(8 * ctx, 8), 8)],
            d_send.at[k], d_recv.at[k], (ctx_peer(k), head),
        )

    def m_slot(source, g):
        return m_all.at[pl.ds(LOCAL * source + GROUP * g, GROUP)]

    def m_near(z):
        return lax.rem(chip + z + CHIPS, CHIPS)

    def m_first(h, step, g, n):
        return remote(
            m_ref.at[h, pl.ds(GROUP * g, GROUP)], m_slot(ctx, g), m_send.at[n], m_recv.at[2 * ctx + g],
            (2 * m_near(step) + h, head),
        )

    def m_sibling(g, n):
        return remote(
            m_ref.at[1 - core, pl.ds(GROUP * g, GROUP)], m_slot(ctx, g), m_send.at[n], m_recv.at[2 * ctx + g],
            (sibling, head),
        )

    def m_next(source, g, step, n):
        return remote(
            m_slot(source, g), m_slot(source, g), m_send.at[n], m_recv.at[2 * source + g],
            (2 * m_near(step) + core, head),
        )

    def w_half(half):
        return w_ref.at[:, pl.ds(pl.multiple_of(half * (MODEL // 2), MODEL // 2), MODEL // 2)]

    def w_copy(k):
        return remote(w_half(core), w_all.at[core, side_y], w_send.at[k], w_recv.at[k], (ctx, y_peer(k)))

    def w_pass(k):
        slot = w_all.at[core, lax.rem(side_y + k, SIDE)]
        return remote(slot, slot, c_send.at[k], c_recv.at[k], (sibling, head))

    row = lax.broadcasted_iota(jnp.int32, (SPAN, SPAN), 0)
    col = lax.broadcasted_iota(jnp.int32, (SPAN, SPAN), 1)
    differ = row ^ col
    incl = row >= col
    strict = row > col
    tri = incl.astype(F32).astype(BF16)
    masks = [((differ >= s) & (differ < 2 * s)).astype(F32).astype(BF16) for s in (2, 4, 8, 16, 32, 64)]
    first = (differ == 1).astype(F32)
    eye = (row == col).astype(F32)
    sent = []
    everything = []

    for load in loads[:5]:
        load.wait()
    for g in range(LOCAL // GROUP):
        chains = []
        for i in range(g * GROUP, (g + 1) * GROUP):
            rows = pl.ds(i * SPAN, SPAN)
            q = q_ref[rows, :]
            k = k_ref[rows, :]
            qf = q.astype(F32)
            kf = k.astype(F32)
            rq = lax.rsqrt(jnp.sum(qf * qf, axis=-1, keepdims=True) + 1e-6) * DK**-0.5
            rk = lax.rsqrt(jnp.sum(kf * kf, axis=-1, keepdims=True) + 1e-6)
            rk_wide = spread_lanes(rk)
            rk_row = rk_wide.T
            both = mm_t(jnp.concatenate([k, q], axis=0), k)
            kk = both[:SPAN] * rk_wide * rk_row
            qk = both[SPAN:] * spread_lanes(rq) * rk_row
            kt = k.T
            shared = (qf * rq, kf, jnp.concatenate([kt, kt], axis=1), rk_wide, kk, qk)
            logits = beta_ref[:, rows].astype(F32)
            decays = decay_ref[:, rows].astype(F32)
            for h in range(HEADS):
                chains.append(
                    block_terms(
                        i, h, q, k, logits[h : h + 1], decays[h : h + 1],
                        v_ref[rows, h * DV : (h + 1) * DV].astype(F32), shared, (tri, strict, incl),
                    )
                )
        for c in chains:
            c["parts"] = split(c["lower"])
            c["inverse"] = eye - c["lower"] * first
        for mask in masks:
            for c in chains:
                c["halves"] = split(c["inverse"])
                off = (c["parts"][0] * mask, c["parts"][1] * mask)
                c["inner"] = product(off, c["halves"])
            for c in chains:
                c["inverse"] = c["inverse"] - product(c["halves"], split(c["inner"]))
        for c in chains:
            c["solved"] = product(split(c["inverse"]), split(c["rhs"]))
        for c in chains:
            tail2 = jnp.concatenate([c["tail"], c["tail"]], axis=1)
            high, low = split(tail2 * c["solved"])
            shift = mm(c["kt2"], jnp.concatenate([high, low], axis=0))
            i, h = c["i"], c["h"]
            m_ref[h, i] = shift[:, DV:].astype(BF16)
            o_ref[h, :, i] = shift[:, :DV].T.reshape(CHIPS, SLICE, DK).astype(BF16)
            d_ref[h * LOCAL + i : h * LOCAL + i + 1, :] = c["decay"]
        everything += chains
        if g == 0:
            pl.semaphore_wait(barrier, PEERS - 1 + 2 * (SIDE - 1))
        firsts = [m_first(h, step, g, g * 5 + n) for n, (h, step) in enumerate(((0, 1), (0, -1), (1, 1), (1, -1)))]
        firsts.append(m_sibling(g, g * 5 + 4))
        for copy in firsts:
            copy.start()
        sent += firsts
        if g == 0:
            for k in range(1, SIDE):
                copy = w_copy(k)
                copy.start()
                sent.append(copy)
            w_own = [
                pltpu.make_async_copy(w_half(half), w_all.at[half, side_y], w_local.at[half]) for half in range(2)
            ]
            for copy in w_own:
                copy.start()

    def send_small(k, carry):
        d_copy(k).start()
        o_copy(k).start()
        return carry

    lax.fori_loop(1, PEERS, send_small, 0)
    m_all[pl.ds(LOCAL * ctx, LOCAL)] = m_ref[core]
    o_all[pl.ds(LOCAL * ctx, LOCAL)] = o_ref[core, chip]
    d_all[pl.ds(pl.multiple_of(8 * ctx, 8), 8), :] = d_ref[...]

    lanes = lax.broadcasted_iota(jnp.int32, (1, SPAN), 1)
    found = jnp.zeros((1, SPAN), jnp.int32)
    for t in range(BLOCKS):
        found = jnp.where(lanes == arr_ref[t], t, found)
    inv_vmem[...] = found
    inv_copy = pltpu.make_async_copy(inv_vmem, inv_ref, inv_sem)
    inv_copy.start()
    bits = jnp.int32(0)
    start = prompt_ref[0]
    for i in range(1, 7):
        bits = bits | (jnp.int32(1) << start)
        start = start + prompt_ref[i]

    for c in everything:
        i, h = c["i"], c["h"]
        local = product(split(c["attend"]), split(c["solved"]))
        lo_ref[h, i] = local[:, :DV]
        ql_ref[h, i] = c["grown"] - local[:, DV:]

    n = 10
    for k in range(1, 5):
        for g in range(LOCAL // GROUP):
            for step in (1, -1):
                for s in range(2):
                    last = 4 if (s == 0) == (step == 1) else 3
                    if k > last:
                        continue
                    source = 2 * m_near(-step * k) + s
                    m_next(source, g, step, 0).wait_recv()
                    if k < last:
                        copy = m_next(source, g, step, n)
                        copy.start()
                        sent.append(copy)
                        n += 1
    for g in range(LOCAL // GROUP):
        m_next(sibling, g, 0, 0).wait_recv()

    def wait_small(k, carry):
        d_copy(k).wait()
        o_copy(k).wait()
        return carry

    lax.fori_loop(1, PEERS, wait_small, 0)
    inv_copy.wait()

    def advance(state, t):
        slot = arr_ref[t]
        stream[t] = state.astype(BF16)
        high, low = split(state)
        moved = mm_t(jnp.concatenate([high, low], axis=0), m_all[slot])
        decay = d_all[pl.ds(lax.div(slot, LOCAL) * 8 + core * LOCAL + lax.rem(slot, LOCAL), 1), :]
        return decay * state - moved[:SLICE] - moved[SLICE:] + o_all[slot].astype(F32)

    def step(t, pair):
        keep = (1 - ((bits >> t) & 1)).astype(F32)
        return advance(keep * pair[0], t), advance(pair[1], t + CHAIN)

    empty = jnp.zeros((SLICE, DK), F32)
    lax.fori_loop(0, CHAIN, step, (empty, empty), unroll=4)

    def place(a, carry):
        states[a] = stream[inv_ref[0, a]]
        return carry

    lax.fori_loop(0, BLOCKS, place, 0, unroll=8)

    def s_rows(h, z):
        return entry.at[h, :, pl.ds(pl.multiple_of(SLICE * z, SLICE), SLICE), :]

    def s_copy(k):
        to = ctx_peer(k)
        return remote(
            states.at[pl.ds(LOCAL * to, LOCAL)], s_rows(core, chip), s_send.at[k], s_recv.at[k], (to, head)
        )

    def s_arrival(k):
        source = lax.rem(ctx - k + PEERS, PEERS)
        return remote(
            states.at[pl.ds(0, LOCAL)], s_rows(lax.rem(source, 2), lax.div(source, 2)),
            s_send.at[k], s_recv.at[k], (ctx, head),
        )

    def send_states(k, carry):
        s_copy(k).start()
        return carry

    lax.fori_loop(1, PEERS, send_states, 0)
    entry[core, :, pl.ds(pl.multiple_of(SLICE * chip, SLICE), SLICE), :] = states[pl.ds(LOCAL * ctx, LOCAL)]
    for copy in w_own:
        copy.wait()
    for k in range(1, SIDE):
        w_copy(SIDE - k).wait_recv()
        copy = w_pass(k)
        copy.start()
        sent.append(copy)
    for load in loads[5:]:
        load.wait()

    def wait_states(k, carry):
        s_copy(k).wait_send()
        s_arrival(k).wait_recv()
        return carry

    lax.fori_loop(1, PEERS, wait_states, 0)

    gain = gain_ref[...]
    for i in range(LOCAL):
        for h in range(HEADS):
            high, low = split(ql_ref[h, i])
            state = entry[h, i]
            both = mm_t(jnp.concatenate([high, low], axis=0), state)
            core_out = both[:SPAN] + both[SPAN:] + lo_ref[h, i]
            scale = lax.rsqrt(jnp.mean(core_out * core_out, axis=-1, keepdims=True) + 1e-6)
            gate = gate_ref[i * SPAN : (i + 1) * SPAN, h * DV : (h + 1) * DV].astype(F32)
            value = core_out * scale * gain * (gate / (1.0 + jnp.exp(-gate)))
            normed[i, :, :, h * DV : (h + 1) * DV] = value.astype(BF16).reshape(SIDE, 32, DV)

    def n_copy(k):
        return remote(
            normed.at[:, lax.rem(side_y + k, SIDE)], rows_all.at[side_y], n_send.at[k], n_recv.at[k], (ctx, y_peer(k))
        )

    for k in range(1, SIDE):
        copy = n_copy(k)
        copy.start()
        sent.append(copy)
    rows_all[side_y] = normed[:, side_y]
    for k in range(1, SIDE):
        w_pass(k).wait_recv()
    for k in range(1, SIDE):
        n_copy(k).wait_recv()

    def p_copy(piece, k):
        return remote(
            part.at[piece, lax.rem(side_x + k, SIDE)], got.at[piece, k],
            p_send.at[piece * SIDE + k], p_recv.at[piece * SIDE + k], (ctx, x_peer(k)),
        )

    left = jnp.concatenate(
        [rows_all[y].reshape(SPAN, HEADS * DV) for y in range(SIDE)], axis=1
    )
    for piece in range(PIECES):
        half, off = divmod(piece * PIECE, MODEL // 2)
        right = w_all[half, :, :, off : off + PIECE].reshape(SIDE * HEADS * DV, PIECE)
        total = mm(left, right)
        part[piece] = total.astype(BF16).reshape(SIDE, 32, PIECE)
        for k in range(1, SIDE):
            copy = p_copy(piece, k)
            copy.start()
            sent.append(copy)
    for piece in range(PIECES):
        total = part[piece, side_x].astype(F32)
        for k in range(1, SIDE):
            p_copy(piece, k).wait_recv()
            total = total + got[piece, k].astype(F32)
        out_ref[:, piece * PIECE : (piece + 1) * PIECE] = total.astype(BF16)
    for copy in sent:
        copy.wait_send()


def per_device(q_rows, k_rows, v_rows, gate_rows, beta_logits, log_decay, norm_gain, out_weight, prompt_blocks, arrival_slot):
    smem = pl.BlockSpec(memory_space=pltpu.SMEM)
    vmem = pl.BlockSpec(memory_space=pltpu.VMEM)
    whole = pl.BlockSpec(memory_space=pl.ANY)
    tokens = LOCAL * SPAN
    dma = pltpu.SemaphoreType.DMA
    return pl.pallas_call(
        main_kernel,
        out_shape=jax.ShapeDtypeStruct((tokens // PEERS, MODEL), BF16),
        in_specs=[smem, smem] + [whole] * 8,
        out_specs=vmem,
        scratch_shapes=[
            pltpu.VMEM((tokens, DK), BF16),
            pltpu.VMEM((tokens, DK), BF16),
            pltpu.VMEM((tokens, HEADS * DV), BF16),
            pltpu.VMEM((tokens, HEADS * DV), BF16),
            pltpu.VMEM((HEADS, tokens), BF16),
            pltpu.VMEM((HEADS, tokens), BF16),
            pltpu.VMEM((1, DV), F32),
            pltpu.VMEM((HEADS, LOCAL, DK, DK), BF16),
            pltpu.VMEM((HEADS, CHIPS, LOCAL, SLICE, DK), BF16),
            pltpu.VMEM((HEADS * LOCAL, DK), F32),
            pltpu.VMEM((HEADS, LOCAL, SPAN, DK), F32),
            pltpu.VMEM((HEADS, LOCAL, SPAN, DV), F32),
            pltpu.VMEM((1, SPAN), jnp.int32),
            pltpu.SMEM((1, SPAN), jnp.int32),
            pltpu.VMEM((BLOCKS, DK, DK), BF16),
            pltpu.VMEM((BLOCKS, SLICE, DK), BF16),
            pltpu.VMEM((PEERS * HEADS * LOCAL, DK), F32),
            pltpu.VMEM((BLOCKS, SLICE, DK), BF16),
            pltpu.VMEM((BLOCKS, SLICE, DK), BF16),
            pltpu.VMEM((HEADS, LOCAL, DV, DK), BF16),
            pltpu.VMEM((LOCAL, SIDE, 32, HEADS * DV), BF16),
            pltpu.VMEM((SIDE, LOCAL, 32, HEADS * DV), BF16),
            pltpu.VMEM((2, SIDE, HEADS * DV, MODEL // 2), BF16),
            pltpu.VMEM((PIECES, SIDE, 32, PIECE), BF16),
            pltpu.VMEM((PIECES, SIDE, 32, PIECE), BF16),
            dma((7,)), dma, dma((SIDE,)), dma((SIDE,)), dma((2,)), dma((SIDE,)), dma((SIDE,)),
            dma((30,)), dma((2 * PEERS,)),
            dma((PEERS,)), dma((PEERS,)), dma((PEERS,)), dma((PEERS,)),
            dma((PEERS,)), dma((PEERS,)), dma((SIDE,)), dma((SIDE,)),
            dma((PIECES * SIDE,)), dma((PIECES * SIDE,)),
        ],
        compiler_params=pltpu.CompilerParams(
            collective_id=0, has_side_effects=True, vmem_limit_bytes=VMEM_LIMIT
        ),
    )(
        arrival_slot, prompt_blocks, q_rows, k_rows, v_rows, gate_rows, beta_logits.T, log_decay.T,
        norm_gain.reshape(1, DV), out_weight,
    )


def solution(mesh):
    in_specs = (
        P("ctx", "head"),
        P("ctx", "head"),
        P("ctx", "head"),
        P("ctx", "head"),
        P("ctx", "head"),
        P("ctx", "head"),
        P(),
        P("head", None),
        P(),
        P(),
    )
    return jax.shard_map(
        per_device, mesh=mesh, in_specs=in_specs, out_specs=P(("ctx", "head"), None), check_vma=False
    )
```

time: 569 us -> 71.7 us (0.13)
  waiting for transfers between devices: 236 us -> 0 us
  starting transfers between devices: 117 us -> 0 us
  other arithmetic: 99.1 us -> 0 us
  Pallas kernels: 0 us -> 70 us
  matrix products: 34 us -> 0 us
  blocking collectives: 33.3 us -> 0 us
  local copies, waits for them, and re-layouts: 32.9 us -> 1.57 us
  between operations: 13.9 us -> 0.01 us
    all_to_all x6 -> x0, waiting for transfers between devices: 128 us -> none  [the longest x1 48.9 us: per_device(): lax.all_to_all(jnp.take(normed, back_from, axis=0), 'ctx', split_axis=0,...]
    reduce_scatter x1 -> x0, waiting for transfers between devices: 79.9 us -> none  [per_device(): lax.psum_scatter(jnp.dot(arrived, out_weight, preferred_element_type=jnp....]
    another operation x3 -> x0, other arithmetic: 79.4 us -> none  [the longest x2 79.3 us: span_terms(): jax.scipy.linalg.solve_triangular(jnp.eye(width, dtype=jnp.float32) + low...]
    pallas_call x0 -> x1, Pallas kernels: none -> 70 us  [per_device(): pl.pallas_call(main_kernel, out_shape=jax.ShapeDtypeStruct((tokens // PEE...]
    ppermute x15 -> x0, starting transfers between devices: 64.5 us -> none  [from_behind(): return lax.ppermute(shard, axis, pairs)]
    all_to_all x6 -> x0, starting transfers between devices: 52.1 us -> none  [the longest x1 26.3 us: per_device(): lax.all_to_all(jnp.take(normed, back_from, axis=0), 'ctx', split_axis=0,...]
    all_to_all x1 -> x0, blocking collectives: 33.3 us -> none  [per_device(): lax.all_to_all(to_buffer(k_rows), 'ctx', split_axis=0, concat_axis=0, til...]
    dot_general x39 -> x0, matrix products: 32 us -> none  [the longest x37 29.1 us: matrix_product(): return jnp.einsum(form, left, right, precision=lax.Precision.HIGHEST)]
  transfers between devices with their start and end apart: 22 -> 0, of which waited for: 21 -> 0; matrix products, arithmetic and copies ran while one was open for 18% -> 0% of each run, Pallas kernels for 0% -> 0%
where the time goes in v1:
time: 71.7 us; the launch traced here: 71.6 us
  Pallas kernels  70 us (98%)
  local copies, waits for them, and re-layouts  1.57 us (2%)
    pallas_call x1, Pallas kernels, per_device(): pl.pallas_call(main_kernel, out_shape=jax.ShapeDtypeStruct((tokens // PEE...  70 us
    unnamed x1, local copies, waits for them, and re-layouts  1.57 us

profile of v1, /device:TPU:1, one launch (start us, length us, event | category | flops | bytes accessed | tf_op | source)
XLA Modules:
  0.0 71.6 jit_solution(10879170402078014120)
XLA Ops:
  0.0 70.0 %shard_map.100 = bf16[32,2048]{1,0:T(8,128)(2,1)} custom-call(s32[64]{0:T(128)} %arr_ref.1, s32[8]{0:T(128)} %prompt_ref.1, bf16[512,128]{1,0:T(8,128)(2,1)} %q_hbm.1, bf16[512,128]{1,0:T(8,128)(2,1)} %k_hbm.1, bf16[512,256]{1,0:T(8,128)(2,1)} %v_hbm.1, bf16[512,256]{1,0:T(8,128)(2,1)} %gate_hbm.1, bf16[2,512]{1,0:T(2,128)(2,1)} %bitcast.3, ...), custom_call_target="tpu_custom_call" | custom-call | tf_op jit(solution)/shard_map/pallas_call | solution.py:436
  70.0 1.6 %copy.12 = bf16[32,2048]{1,0:T(8,128)(2,1)} copy(bf16[32,2048]{1,0:T(8,128)(2,1)} %shard_map.100) | data formatting | bytes 262144

commit v2 on v1

--- a/solution.py
+++ b/solution.py
@@ -87,7 +87,7 @@
     m_ref, o_ref, d_ref, ql_ref, lo_ref, inv_vmem, inv_ref,
     m_all, o_all, d_all, stream, states, entry, normed, rows_all, w_all, part, got,
     in_sem, inv_sem, w_send, w_recv, w_local, c_send, c_recv, m_send, m_recv, o_send, o_recv, d_send, d_recv,
-    s_send, s_recv, n_send, n_recv, p_send, p_recv,
+    s_send, s_recv, n_send, n_recv, r_send, r_recv, p_send, p_recv,
 ):
     ctx = lax.axis_index("ctx")
     head = lax.axis_index("head")
@@ -171,11 +171,15 @@
     def w_half(half):
         return w_ref.at[:, pl.ds(pl.multiple_of(half * (MODEL // 2), MODEL // 2), MODEL // 2)]
 
+    def pick(over_x, over_y):
+        return core * over_x + (1 - core) * over_y
+
     def w_copy(k):
-        return remote(w_half(core), w_all.at[core, side_y], w_send.at[k], w_recv.at[k], (ctx, y_peer(k)))
+        to = pick(x_peer(k), y_peer(k))
+        return remote(w_half(core), w_all.at[core, pick(side_x, side_y)], w_send.at[k], w_recv.at[k], (ctx, to))
 
     def w_pass(k):
-        slot = w_all.at[core, lax.rem(side_y + k, SIDE)]
+        slot = w_all.at[core, lax.rem(pick(side_x, side_y) + k, SIDE)]
         return remote(slot, slot, c_send.at[k], c_recv.at[k], (sibling, head))
 
     row = lax.broadcasted_iota(jnp.int32, (SPAN, SPAN), 0)
@@ -235,7 +239,7 @@
             high, low = split(tail2 * c["solved"])
             shift = mm(c["kt2"], jnp.concatenate([high, low], axis=0))
             i, h = c["i"], c["h"]
-            m_ref[h, i] = shift[:, DV:].astype(BF16)
+            m_ref[h, i] = shift[:, DV:].T.astype(BF16)
             o_ref[h, :, i] = shift[:, :DV].T.reshape(CHIPS, SLICE, DK).astype(BF16)
             d_ref[h * LOCAL + i : h * LOCAL + i + 1, :] = c["decay"]
         everything += chains
@@ -252,7 +256,8 @@
                 copy.start()
                 sent.append(copy)
             w_own = [
-                pltpu.make_async_copy(w_half(half), w_all.at[half, side_y], w_local.at[half]) for half in range(2)
+                pltpu.make_async_copy(w_half(half), w_all.at[half, side], w_local.at[half])
+                for half, side in enumerate((side_y, side_x))
             ]
             for copy in w_own:
                 copy.start()
@@ -316,7 +321,7 @@
         slot = arr_ref[t]
         stream[t] = state.astype(BF16)
         high, low = split(state)
-        moved = mm_t(jnp.concatenate([high, low], axis=0), m_all[slot])
+        moved = mm(jnp.concatenate([high, low], axis=0), m_all[slot])
         decay = d_all[pl.ds(lax.div(slot, LOCAL) * 8 + core * LOCAL + lax.rem(slot, LOCAL), 1), :]
         return decay * state - moved[:SLICE] - moved[SLICE:] + o_all[slot].astype(F32)
 
@@ -372,6 +377,20 @@
 
     lax.fori_loop(1, PEERS, wait_states, 0)
 
+    def n_copy(i, k):
+        return remote(
+            normed.at[i, lax.rem(side_y + k, SIDE)], rows_all.at[0, side_y, i],
+            n_send.at[i * SIDE + k], n_recv.at[i * SIDE + k], (ctx, y_peer(k)),
+        )
+
+    def r_copy(i):
+        return remote(
+            normed.at[i], rows_all.at[1, side_x], r_send.at[i], r_recv.at[side_x], (ctx, i * SIDE + side_y)
+        )
+
+    def r_arrival(x):
+        return remote(normed.at[x], rows_all.at[1, x], r_send.at[x], r_recv.at[x], (ctx, head))
+
     gain = gain_ref[...]
     for i in range(LOCAL):
         for h in range(HEADS):
@@ -383,33 +402,46 @@
             gate = gate_ref[i * SPAN : (i + 1) * SPAN, h * DV : (h + 1) * DV].astype(F32)
             value = core_out * scale * gain * (gate / (1.0 + jnp.exp(-gate)))
             normed[i, :, :, h * DV : (h + 1) * DV] = value.astype(BF16).reshape(SIDE, 32, DV)
-
-    def n_copy(k):
-        return remote(
-            normed.at[:, lax.rem(side_y + k, SIDE)], rows_all.at[side_y], n_send.at[k], n_recv.at[k], (ctx, y_peer(k))
-        )
-
-    for k in range(1, SIDE):
-        copy = n_copy(k)
-        copy.start()
-        sent.append(copy)
-    rows_all[side_y] = normed[:, side_y]
+        for k in range(1, SIDE):
+            copy = n_copy(i, k)
+            copy.start()
+            sent.append(copy)
+
+        @pl.when(i != side_x)
+        def _():
+            r_copy(i).start()
+
+    rows_all[0, side_y] = normed[:, side_y]
+    rows_all[1, side_x] = normed[side_x]
     for k in range(1, SIDE):
         w_pass(k).wait_recv()
-    for k in range(1, SIDE):
-        n_copy(k).wait_recv()
+    for i in range(LOCAL):
+        for k in range(1, SIDE):
+            n_copy(i, k).wait_recv()
 
     def p_copy(piece, k):
-        return remote(
-            part.at[piece, lax.rem(side_x + k, SIDE)], got.at[piece, k],
-            p_send.at[piece * SIDE + k], p_recv.at[piece * SIDE + k], (ctx, x_peer(k)),
-        )
-
-    left = jnp.concatenate(
-        [rows_all[y].reshape(SPAN, HEADS * DV) for y in range(SIDE)], axis=1
-    )
+        if piece < PIECES // 2:
+            source, to = lax.rem(side_x + k, SIDE), x_peer(k)
+        else:
+            source, to = lax.rem(side_y + k, SIDE), y_peer(k)
+        return remote(
+            part.at[piece, source], got.at[piece, k],
+            p_send.at[piece * SIDE + k], p_recv.at[piece * SIDE + k], (ctx, to),
+        )
+
     for piece in range(PIECES):
         half, off = divmod(piece * PIECE, MODEL // 2)
+        if piece == PIECES // 2:
+            for x in range(SIDE):
+
+                @pl.when(x != side_x)
+                def _():
+                    r_arrival(x).wait_recv()
+
+        if off == 0:
+            left = jnp.concatenate(
+                [rows_all[half, n].reshape(SPAN, HEADS * DV) for n in range(SIDE)], axis=1
+            )
         right = w_all[half, :, :, off : off + PIECE].reshape(SIDE * HEADS * DV, PIECE)
         total = mm(left, right)
         part[piece] = total.astype(BF16).reshape(SIDE, 32, PIECE)
@@ -418,11 +450,17 @@
             copy.start()
             sent.append(copy)
     for piece in range(PIECES):
-        total = part[piece, side_x].astype(F32)
+        total = part[piece, side_x if piece < PIECES // 2 else side_y].astype(F32)
         for k in range(1, SIDE):
             p_copy(piece, k).wait_recv()
             total = total + got[piece, k].astype(F32)
         out_ref[:, piece * PIECE : (piece + 1) * PIECE] = total.astype(BF16)
+    for i in range(LOCAL):
+
+        @pl.when(i != side_x)
+        def _():
+            r_copy(i).wait_send()
+
     for copy in sent:
         copy.wait_send()
 
@@ -435,7 +473,7 @@
     dma = pltpu.SemaphoreType.DMA
     return pl.pallas_call(
         main_kernel,
-        out_shape=jax.ShapeDtypeStruct((tokens // PEERS, MODEL), BF16),
+        out_shape=pltpu.VMEM((tokens // PEERS, MODEL), BF16),
         in_specs=[smem, smem] + [whole] * 8,
         out_specs=vmem,
         scratch_shapes=[
@@ -460,14 +498,14 @@
             pltpu.VMEM((BLOCKS, SLICE, DK), BF16),
             pltpu.VMEM((HEADS, LOCAL, DV, DK), BF16),
             pltpu.VMEM((LOCAL, SIDE, 32, HEADS * DV), BF16),
-            pltpu.VMEM((SIDE, LOCAL, 32, HEADS * DV), BF16),
+            pltpu.VMEM((2, SIDE, LOCAL, 32, HEADS * DV), BF16),
             pltpu.VMEM((2, SIDE, HEADS * DV, MODEL // 2), BF16),
             pltpu.VMEM((PIECES, SIDE, 32, PIECE), BF16),
             pltpu.VMEM((PIECES, SIDE, 32, PIECE), BF16),
             dma((7,)), dma, dma((SIDE,)), dma((SIDE,)), dma((2,)), dma((SIDE,)), dma((SIDE,)),
             dma((30,)), dma((2 * PEERS,)),
             dma((PEERS,)), dma((PEERS,)), dma((PEERS,)), dma((PEERS,)),
-            dma((PEERS,)), dma((PEERS,)), dma((SIDE,)), dma((SIDE,)),
+            dma((PEERS,)), dma((PEERS,)), dma((LOCAL * SIDE,)), dma((LOCAL * SIDE,)), dma((SIDE,)), dma((SIDE,)),
             dma((PIECES * SIDE,)), dma((PIECES * SIDE,)),
         ],
         compiler_params=pltpu.CompilerParams(

time: 71.7 us -> 67.8 us (0.946)
  Pallas kernels: 70 us -> 67 us
  local copies, waits for them, and re-layouts: 1.57 us -> 0.66 us
    pallas_call x1, Pallas kernels: 70 us -> 67 us  [per_device(): pl.pallas_call(main_kernel, out_shape=pltpu.VMEM((tokens // PEERS, MODEL)...]
    unnamed x1, local copies, waits for them, and re-layouts: 1.57 us -> 0.66 us
where the time goes in v2:
time: 67.8 us; the launch traced here: 67.7 us
  Pallas kernels  67 us (99%)
    pallas_call x1, Pallas kernels, per_device(): pl.pallas_call(main_kernel, out_shape=pltpu.VMEM((tokens // PEERS, MODEL)...  67 us

profile of v2, /device:TPU:1, one launch (start us, length us, event | category | flops | bytes accessed | tf_op | source)
XLA Modules:
  0.0 67.7 jit_solution(14919076667867099100)
XLA Ops:
  0.0 67.0 %shard_map.100 = bf16[32,2048]{1,0:T(8,128)(2,1)S(1)} custom-call(s32[64]{0:T(128)} %arr_ref.1, s32[8]{0:T(128)} %prompt_ref.1, bf16[512,128]{1,0:T(8,128)(2,1)} %q_hbm.1, bf16[512,128]{1,0:T(8,128)(2,1)} %k_hbm.1, bf16[512,256]{1,0:T(8,128)(2,1)} %v_hbm.1, bf16[512,256]{1,0:T(8,128)(2,1)} %gate_hbm.1, bf16[2,512]{1,0:T(2,128)(2,1)} %bitcast.3, ...), custom_call_target="tpu_custom_call" | custom-call | tf_op jit(solution)/shard_map/pallas_call | solution.py:474
  67.0 0.7 copy.12

commit v3 on v2

--- a/solution.py
+++ b/solution.py
@@ -86,7 +86,7 @@
     q_ref, k_ref, v_ref, gate_ref, beta_ref, decay_ref, gain_ref,
     m_ref, o_ref, d_ref, ql_ref, lo_ref, inv_vmem, inv_ref,
     m_all, o_all, d_all, stream, states, entry, normed, rows_all, w_all, part, got,
-    in_sem, inv_sem, w_send, w_recv, w_local, c_send, c_recv, m_send, m_recv, o_send, o_recv, d_send, d_recv,
+    in_sem, inv_sem, w_send, w_recv, w_local, c_send, c_recv, m_send, m_recv, o_send, o_recv,
     s_send, s_recv, n_send, n_recv, r_send, r_recv, p_send, p_recv,
 ):
     ctx = lax.axis_index("ctx")
@@ -106,10 +106,6 @@
 
     barrier = pltpu.get_barrier_semaphore()
 
-    def greet(k, carry):
-        pl.semaphore_signal(barrier, inc=1, device_id=(ctx_peer(k), head), device_id_type=MESH)
-        return carry
-
     loads = [
         pltpu.make_async_copy(src, dst, in_sem.at[n])
         for n, (src, dst) in enumerate(
@@ -121,7 +117,8 @@
     ]
     for load in loads:
         load.start()
-    lax.fori_loop(1, PEERS, greet, 0)
+    for k in range(1, PEERS):
+        pl.semaphore_signal(barrier, inc=1, device_id=(ctx_peer(k), head), device_id_type=MESH)
     for k in range(1, SIDE):
         pl.semaphore_signal(barrier, inc=1, device_id=(ctx, y_peer(k)), device_id_type=MESH)
         pl.semaphore_signal(barrier, inc=1, device_id=(ctx, x_peer(k)), device_id_type=MESH)
@@ -131,18 +128,15 @@
             src_ref=src, dst_ref=dst, send_sem=send, recv_sem=recv, device_id=target, device_id_type=MESH
         )
 
+    def finish_sends(ref, sem):
+        remote(ref, ref, sem, sem, (ctx, head)).wait_send()
+
+    def finish_arrivals(ref, sem):
+        remote(ref, ref, sem, sem, (ctx, head)).wait_recv()
+
     def o_copy(k):
         to = ctx_peer(k)
-        return remote(
-            o_ref.at[lax.rem(to, 2), lax.div(to, 2)], o_all.at[pl.ds(LOCAL * ctx, LOCAL)],
-            o_send.at[k], o_recv.at[k], (to, head),
-        )
-
-    def d_copy(k):
-        return remote(
-            d_ref, d_all.at[pl.ds(pl.multiple_of(8 * ctx, 8), 8)],
-            d_send.at[k], d_recv.at[k], (ctx_peer(k), head),
-        )
+        return remote(o_ref.at[lax.rem(to, 2), lax.div(to, 2)], o_all.at[ctx], o_send, o_recv, (to, head))
 
     def m_slot(source, g):
         return m_all.at[pl.ds(LOCAL * source + GROUP * g, GROUP)]
@@ -150,23 +144,41 @@
     def m_near(z):
         return lax.rem(chip + z + CHIPS, CHIPS)
 
-    def m_first(h, step, g, n):
+    def m_first(h, step, g):
         return remote(
-            m_ref.at[h, pl.ds(GROUP * g, GROUP)], m_slot(ctx, g), m_send.at[n], m_recv.at[2 * ctx + g],
+            m_ref.at[h, pl.ds(GROUP * g, GROUP)], m_slot(ctx, g), m_send, m_recv.at[2 * ctx + g],
             (2 * m_near(step) + h, head),
         )
 
-    def m_sibling(g, n):
+    def m_sibling(g):
         return remote(
-            m_ref.at[1 - core, pl.ds(GROUP * g, GROUP)], m_slot(ctx, g), m_send.at[n], m_recv.at[2 * ctx + g],
+            m_ref.at[1 - core, pl.ds(GROUP * g, GROUP)], m_slot(ctx, g), m_send, m_recv.at[2 * ctx + g],
             (sibling, head),
         )
 
-    def m_next(source, g, step, n):
+    def m_next(source, g, step):
         return remote(
-            m_slot(source, g), m_slot(source, g), m_send.at[n], m_recv.at[2 * source + g],
+            m_slot(source, g), m_slot(source, g), m_send, m_recv.at[2 * source + g],
             (2 * m_near(step) + core, head),
         )
+
+    def forward(k, g):
+        for step in (1, -1):
+            for s in range(2):
+                last = 4 if (s == 0) == (step == 1) else 3
+                if k > last:
+                    continue
+                source = 2 * m_near(-step * k) + s
+                m_next(source, g, step).wait_recv()
+                if k < last:
+                    m_next(source, g, step).start()
+
+    def attend_locally(chains):
+        for c in chains:
+            i, h = c["i"], c["h"]
+            local = product(split(c["attend"]), split(c["solved"]))
+            lo_ref[h, i] = local[:, :DV]
+            ql_ref[h, i] = c["grown"] - local[:, DV:]
 
     def w_half(half):
         return w_ref.at[:, pl.ds(pl.multiple_of(half * (MODEL // 2), MODEL // 2), MODEL // 2)]
@@ -176,11 +188,11 @@
 
     def w_copy(k):
         to = pick(x_peer(k), y_peer(k))
-        return remote(w_half(core), w_all.at[core, pick(side_x, side_y)], w_send.at[k], w_recv.at[k], (ctx, to))
+        return remote(w_half(core), w_all.at[core, pick(side_x, side_y)], w_send, w_recv, (ctx, to))
 
     def w_pass(k):
         slot = w_all.at[core, lax.rem(pick(side_x, side_y) + k, SIDE)]
-        return remote(slot, slot, c_send.at[k], c_recv.at[k], (sibling, head))
+        return remote(slot, slot, c_send, c_recv, (sibling, head))
 
     row = lax.broadcasted_iota(jnp.int32, (SPAN, SPAN), 0)
     col = lax.broadcasted_iota(jnp.int32, (SPAN, SPAN), 1)
@@ -191,7 +203,7 @@
     masks = [((differ >= s) & (differ < 2 * s)).astype(F32).astype(BF16) for s in (2, 4, 8, 16, 32, 64)]
     first = (differ == 1).astype(F32)
     eye = (row == col).astype(F32)
-    sent = []
+    d_ref[...] = jnp.zeros((HEADS, SLICE, DK), F32)
     everything = []
 
     for load in loads[:5]:
@@ -241,20 +253,18 @@
             i, h = c["i"], c["h"]
             m_ref[h, i] = shift[:, DV:].T.astype(BF16)
             o_ref[h, :, i] = shift[:, :DV].T.reshape(CHIPS, SLICE, DK).astype(BF16)
-            d_ref[h * LOCAL + i : h * LOCAL + i + 1, :] = c["decay"]
+            decay = c["decay"].astype(BF16).astype(F32)
+            d_ref[h, i : i + 1, :] = decay
+            d_ref[h, 8 + i : 9 + i, :] = c["decay"] - decay
         everything += chains
         if g == 0:
             pl.semaphore_wait(barrier, PEERS - 1 + 2 * (SIDE - 1))
-        firsts = [m_first(h, step, g, g * 5 + n) for n, (h, step) in enumerate(((0, 1), (0, -1), (1, 1), (1, -1)))]
-        firsts.append(m_sibling(g, g * 5 + 4))
-        for copy in firsts:
-            copy.start()
-        sent += firsts
+        for h, step in ((0, 1), (0, -1), (1, 1), (1, -1)):
+            m_first(h, step, g).start()
+        m_sibling(g).start()
         if g == 0:
             for k in range(1, SIDE):
-                copy = w_copy(k)
-                copy.start()
-                sent.append(copy)
+                w_copy(k).start()
             w_own = [
                 pltpu.make_async_copy(w_half(half), w_all.at[half, side], w_local.at[half])
                 for half, side in enumerate((side_y, side_x))
@@ -262,15 +272,18 @@
             for copy in w_own:
                 copy.start()
 
-    def send_small(k, carry):
-        d_copy(k).start()
+    forward(1, 0)
+    for h in range(HEADS):
+        o_ref[h, :, LOCAL] = jnp.broadcast_to(d_ref[h].astype(BF16), (CHIPS, SLICE, DK))
+    for k in range(1, PEERS):
         o_copy(k).start()
-        return carry
-
-    lax.fori_loop(1, PEERS, send_small, 0)
     m_all[pl.ds(LOCAL * ctx, LOCAL)] = m_ref[core]
-    o_all[pl.ds(LOCAL * ctx, LOCAL)] = o_ref[core, chip]
-    d_all[pl.ds(pl.multiple_of(8 * ctx, 8), 8), :] = d_ref[...]
+    o_all[ctx] = o_ref[core, chip]
+    forward(1, 1)
+    attend_locally(everything[: len(everything) // 2])
+    forward(2, 0)
+    attend_locally(everything[len(everything) // 2 :])
+    forward(2, 1)
 
     lanes = lax.broadcasted_iota(jnp.int32, (1, SPAN), 1)
     found = jnp.zeros((1, SPAN), jnp.int32)
@@ -285,36 +298,15 @@
         bits = bits | (jnp.int32(1) << start)
         start = start + prompt_ref[i]
 
-    for c in everything:
-        i, h = c["i"], c["h"]
-        local = product(split(c["attend"]), split(c["solved"]))
-        lo_ref[h, i] = local[:, :DV]
-        ql_ref[h, i] = c["grown"] - local[:, DV:]
-
-    n = 10
-    for k in range(1, 5):
+    for k in (3, 4):
         for g in range(LOCAL // GROUP):
-            for step in (1, -1):
-                for s in range(2):
-                    last = 4 if (s == 0) == (step == 1) else 3
-                    if k > last:
-                        continue
-                    source = 2 * m_near(-step * k) + s
-                    m_next(source, g, step, 0).wait_recv()
-                    if k < last:
-                        copy = m_next(source, g, step, n)
-                        copy.start()
-                        sent.append(copy)
-                        n += 1
+            forward(k, g)
     for g in range(LOCAL // GROUP):
-        m_next(sibling, g, 0, 0).wait_recv()
-
-    def wait_small(k, carry):
-        d_copy(k).wait()
-        o_copy(k).wait()
-        return carry
-
-    lax.fori_loop(1, PEERS, wait_small, 0)
+        m_next(sibling, g, 0).wait_recv()
+    finish_arrivals(o_all.at[pl.ds(0, PEERS - 1)], o_recv)
+    for source in range(PEERS):
+        tile = o_all[source, LOCAL].astype(F32)
+        d_all[source * 8 : source * 8 + 8, :] = tile[:8] + tile[8:]
     inv_copy.wait()
 
     def advance(state, t):
@@ -322,15 +314,16 @@
         stream[t] = state.astype(BF16)
         high, low = split(state)
         moved = mm(jnp.concatenate([high, low], axis=0), m_all[slot])
-        decay = d_all[pl.ds(lax.div(slot, LOCAL) * 8 + core * LOCAL + lax.rem(slot, LOCAL), 1), :]
-        return decay * state - moved[:SLICE] - moved[SLICE:] + o_all[slot].astype(F32)
+        source, i = lax.div(slot, LOCAL), lax.rem(slot, LOCAL)
+        decay = d_all[pl.ds(source * 8 + i, 1), :]
+        return decay * state + o_all[source, i].astype(F32) - (moved[:SLICE] + moved[SLICE:])
 
     def step(t, pair):
         keep = (1 - ((bits >> t) & 1)).astype(F32)
         return advance(keep * pair[0], t), advance(pair[1], t + CHAIN)
 
     empty = jnp.zeros((SLICE, DK), F32)
-    lax.fori_loop(0, CHAIN, step, (empty, empty), unroll=4)
+    lax.fori_loop(0, CHAIN, step, (empty, empty), unroll=16)
 
     def place(a, carry):
         states[a] = stream[inv_ref[0, a]]
@@ -343,53 +336,27 @@
 
     def s_copy(k):
         to = ctx_peer(k)
-        return remote(
-            states.at[pl.ds(LOCAL * to, LOCAL)], s_rows(core, chip), s_send.at[k], s_recv.at[k], (to, head)
-        )
-
-    def s_arrival(k):
-        source = lax.rem(ctx - k + PEERS, PEERS)
-        return remote(
-            states.at[pl.ds(0, LOCAL)], s_rows(lax.rem(source, 2), lax.div(source, 2)),
-            s_send.at[k], s_recv.at[k], (ctx, head),
-        )
-
-    def send_states(k, carry):
+        return remote(states.at[pl.ds(LOCAL * to, LOCAL)], s_rows(core, chip), s_send, s_recv, (to, head))
+
+    for k in range(1, PEERS):
         s_copy(k).start()
-        return carry
-
-    lax.fori_loop(1, PEERS, send_states, 0)
     entry[core, :, pl.ds(pl.multiple_of(SLICE * chip, SLICE), SLICE), :] = states[pl.ds(LOCAL * ctx, LOCAL)]
     for copy in w_own:
         copy.wait()
+    finish_arrivals(w_all.at[0, pl.ds(0, SIDE - 1)], w_recv)
     for k in range(1, SIDE):
-        w_copy(SIDE - k).wait_recv()
-        copy = w_pass(k)
-        copy.start()
-        sent.append(copy)
+        w_pass(k).start()
     for load in loads[5:]:
         load.wait()
-
-    def wait_states(k, carry):
-        s_copy(k).wait_send()
-        s_arrival(k).wait_recv()
-        return carry
-
-    lax.fori_loop(1, PEERS, wait_states, 0)
-
-    def n_copy(i, k):
+    finish_arrivals(states.at[pl.ds(0, LOCAL * (PEERS - 1))], s_recv)
+
+    def n_copy(k):
         return remote(
-            normed.at[i, lax.rem(side_y + k, SIDE)], rows_all.at[0, side_y, i],
-            n_send.at[i * SIDE + k], n_recv.at[i * SIDE + k], (ctx, y_peer(k)),
+            normed.at[:, lax.rem(side_y + k, SIDE)], rows_all.at[0, side_y], n_send, n_recv, (ctx, y_peer(k))
         )
 
     def r_copy(i):
-        return remote(
-            normed.at[i], rows_all.at[1, side_x], r_send.at[i], r_recv.at[side_x], (ctx, i * SIDE + side_y)
-        )
-
-    def r_arrival(x):
-        return remote(normed.at[x], rows_all.at[1, x], r_send.at[x], r_recv.at[x], (ctx, head))
+        return remote(normed.at[i], rows_all.at[1, side_x], r_send, r_recv, (ctx, i * SIDE + side_y))
 
     gain = gain_ref[...]
     for i in range(LOCAL):
@@ -402,22 +369,17 @@
             gate = gate_ref[i * SPAN : (i + 1) * SPAN, h * DV : (h + 1) * DV].astype(F32)
             value = core_out * scale * gain * (gate / (1.0 + jnp.exp(-gate)))
             normed[i, :, :, h * DV : (h + 1) * DV] = value.astype(BF16).reshape(SIDE, 32, DV)
-        for k in range(1, SIDE):
-            copy = n_copy(i, k)
-            copy.start()
-            sent.append(copy)
 
         @pl.when(i != side_x)
         def _():
             r_copy(i).start()
 
+    for k in range(1, SIDE):
+        n_copy(k).start()
     rows_all[0, side_y] = normed[:, side_y]
     rows_all[1, side_x] = normed[side_x]
-    for k in range(1, SIDE):
-        w_pass(k).wait_recv()
-    for i in range(LOCAL):
-        for k in range(1, SIDE):
-            n_copy(i, k).wait_recv()
+    finish_arrivals(w_all.at[0, pl.ds(0, SIDE - 1)], c_recv)
+    finish_arrivals(rows_all.at[0, pl.ds(0, SIDE - 1)], n_recv)
 
     def p_copy(piece, k):
         if piece < PIECES // 2:
@@ -426,18 +388,13 @@
             source, to = lax.rem(side_y + k, SIDE), y_peer(k)
         return remote(
             part.at[piece, source], got.at[piece, k],
-            p_send.at[piece * SIDE + k], p_recv.at[piece * SIDE + k], (ctx, to),
+            p_send, p_recv.at[piece], (ctx, to),
         )
 
     for piece in range(PIECES):
         half, off = divmod(piece * PIECE, MODEL // 2)
         if piece == PIECES // 2:
-            for x in range(SIDE):
-
-                @pl.when(x != side_x)
-                def _():
-                    r_arrival(x).wait_recv()
-
+            finish_arrivals(rows_all.at[1, pl.ds(0, SIDE - 1)], r_recv)
         if off == 0:
             left = jnp.concatenate(
                 [rows_all[half, n].reshape(SPAN, HEADS * DV) for n in range(SIDE)], axis=1
@@ -446,23 +403,21 @@
         total = mm(left, right)
         part[piece] = total.astype(BF16).reshape(SIDE, 32, PIECE)
         for k in range(1, SIDE):
-            copy = p_copy(piece, k)
-            copy.start()
-            sent.append(copy)
+            p_copy(piece, k).start()
     for piece in range(PIECES):
         total = part[piece, side_x if piece < PIECES // 2 else side_y].astype(F32)
+        finish_arrivals(got.at[piece, pl.ds(1, SIDE - 1)], p_recv.at[piece])
         for k in range(1, SIDE):
-            p_copy(piece, k).wait_recv()
             total = total + got[piece, k].astype(F32)
         out_ref[:, piece * PIECE : (piece + 1) * PIECE] = total.astype(BF16)
-    for i in range(LOCAL):
-
-        @pl.when(i != side_x)
-        def _():
-            r_copy(i).wait_send()
-
-    for copy in sent:
-        copy.wait_send()
+    finish_sends(m_all.at[pl.ds(0, LOCAL * (PEERS - 1))], m_send)
+    finish_sends(o_all.at[pl.ds(0, PEERS - 1)], o_send)
+    finish_sends(states.at[pl.ds(0, LOCAL * (PEERS - 1))], s_send)
+    finish_sends(w_all.at[0, pl.ds(0, SIDE - 1)], w_send)
+    finish_sends(w_all.at[0, pl.ds(0, SIDE - 1)], c_send)
+    finish_sends(rows_all.at[0, pl.ds(0, SIDE - 1)], n_send)
+    finish_sends(rows_all.at[1, pl.ds(0, SIDE - 1)], r_send)
+    finish_sends(part.at[pl.ds(0, PIECES - 1)], p_send)
 
 
 def per_device(q_rows, k_rows, v_rows, gate_rows, beta_logits, log_decay, norm_gain, out_weight, prompt_blocks, arrival_slot):
@@ -485,15 +440,15 @@
             pltpu.VMEM((HEADS, tokens), BF16),
             pltpu.VMEM((1, DV), F32),
             pltpu.VMEM((HEADS, LOCAL, DK, DK), BF16),
-            pltpu.VMEM((HEADS, CHIPS, LOCAL, SLICE, DK), BF16),
-            pltpu.VMEM((HEADS * LOCAL, DK), F32),
+            pltpu.VMEM((HEADS, CHIPS, LOCAL + 1, SLICE, DK), BF16),
+            pltpu.VMEM((HEADS, SLICE, DK), F32),
             pltpu.VMEM((HEADS, LOCAL, SPAN, DK), F32),
             pltpu.VMEM((HEADS, LOCAL, SPAN, DV), F32),
             pltpu.VMEM((1, SPAN), jnp.int32),
             pltpu.SMEM((1, SPAN), jnp.int32),
             pltpu.VMEM((BLOCKS, DK, DK), BF16),
-            pltpu.VMEM((BLOCKS, SLICE, DK), BF16),
-            pltpu.VMEM((PEERS * HEADS * LOCAL, DK), F32),
+            pltpu.VMEM((PEERS, LOCAL + 1, SLICE, DK), BF16),
+            pltpu.VMEM((PEERS * 8, DK), F32),
             pltpu.VMEM((BLOCKS, SLICE, DK), BF16),
             pltpu.VMEM((BLOCKS, SLICE, DK), BF16),
             pltpu.VMEM((HEADS, LOCAL, DV, DK), BF16),
@@ -502,11 +457,9 @@
             pltpu.VMEM((2, SIDE, HEADS * DV, MODEL // 2), BF16),
             pltpu.VMEM((PIECES, SIDE, 32, PIECE), BF16),
             pltpu.VMEM((PIECES, SIDE, 32, PIECE), BF16),
-            dma((7,)), dma, dma((SIDE,)), dma((SIDE,)), dma((2,)), dma((SIDE,)), dma((SIDE,)),
-            dma((30,)), dma((2 * PEERS,)),
-            dma((PEERS,)), dma((PEERS,)), dma((PEERS,)), dma((PEERS,)),
-            dma((PEERS,)), dma((PEERS,)), dma((LOCAL * SIDE,)), dma((LOCAL * SIDE,)), dma((SIDE,)), dma((SIDE,)),
-            dma((PIECES * SIDE,)), dma((PIECES * SIDE,)),
+            dma((7,)), dma, dma, dma, dma((2,)), dma, dma,
+            dma, dma((2 * PEERS,)), dma, dma,
+            dma, dma, dma, dma, dma, dma, dma, dma((PIECES,)),
         ],
         compiler_params=pltpu.CompilerParams(
             collective_id=0, has_side_effects=True, vmem_limit_bytes=VMEM_LIMIT

time: 67.8 us -> 67.1 us (0.990)
  Pallas kernels: 67 us -> 66.3 us
    pallas_call x1, Pallas kernels: 67 us -> 66.3 us  [per_device(): pl.pallas_call(main_kernel, out_shape=pltpu.VMEM((tokens // PEERS, MODEL)...]
where the time goes in v3:
time: 67.1 us; the launch traced here: 67 us
  Pallas kernels  66.3 us (99%)
    pallas_call x1, Pallas kernels, per_device(): pl.pallas_call(main_kernel, out_shape=pltpu.VMEM((tokens // PEERS, MODEL)...  66.3 us

profile of v3, /device:TPU:1, one launch (start us, length us, event | category | flops | bytes accessed | tf_op | source)
XLA Modules:
  0.0 67.0 jit_solution(10255960767819504666)
XLA Ops:
  0.0 66.3 %shard_map.100 = bf16[32,2048]{1,0:T(8,128)(2,1)S(1)} custom-call(s32[64]{0:T(128)} %arr_ref.1, s32[8]{0:T(128)} %prompt_ref.1, bf16[512,128]{1,0:T(8,128)(2,1)} %q_hbm.1, bf16[512,128]{1,0:T(8,128)(2,1)} %k_hbm.1, bf16[512,256]{1,0:T(8,128)(2,1)} %v_hbm.1, bf16[512,256]{1,0:T(8,128)(2,1)} %gate_hbm.1, bf16[2,512]{1,0:T(2,128)(2,1)} %bitcast.3, ...), custom_call_target="tpu_custom_call" | custom-call | tf_op jit(solution)/shard_map/pallas_call | solution.py:429
  66.3 0.7 copy.12

commit v4 on v3

--- a/solution.py
+++ b/solution.py
@@ -12,7 +12,8 @@
 LOCAL = 4
 PEERS = 16
 CHIPS = 8
-SLICE = 16
+SLICE = 32
+ROOTS = 4
 BLOCKS = 64
 CHAIN = 32
 SIDE = 4
@@ -86,7 +87,7 @@
     q_ref, k_ref, v_ref, gate_ref, beta_ref, decay_ref, gain_ref,
     m_ref, o_ref, d_ref, ql_ref, lo_ref, inv_vmem, inv_ref,
     m_all, o_all, d_all, stream, states, entry, normed, rows_all, w_all, part, got,
-    in_sem, inv_sem, w_send, w_recv, w_local, c_send, c_recv, m_send, m_recv, o_send, o_recv,
+    in_sem, inv_sem, w_send, w_recv, w_local, c_send, c_recv, m_send, m_recv, m_pass, o_send, o_recv,
     s_send, s_recv, n_send, n_recv, r_send, r_recv, p_send, p_recv,
 ):
     ctx = lax.axis_index("ctx")
@@ -134,44 +135,50 @@
     def finish_arrivals(ref, sem):
         remote(ref, ref, sem, sem, (ctx, head)).wait_recv()
 
-    def o_copy(k):
-        to = ctx_peer(k)
-        return remote(o_ref.at[lax.rem(to, 2), lax.div(to, 2)], o_all.at[ctx], o_send, o_recv, (to, head))
+    root_head, root_chip = lax.div(chip, CHIPS // 2), lax.rem(chip, CHIPS // 2)
+    is_root = root_chip < 2
+    column = 2 * root_chip + core
+
+    def o_copy(h, r):
+        return remote(o_ref.at[h, r], o_all.at[ctx], o_send, o_recv, (PEERS // 2 * h + r, head))
+
+    def root_of(h):
+        return (ctx >= PEERS // 2 * h) & (ctx < PEERS // 2 * h + ROOTS)
 
     def m_slot(source, g):
         return m_all.at[pl.ds(LOCAL * source + GROUP * g, GROUP)]
 
-    def m_near(z):
-        return lax.rem(chip + z + CHIPS, CHIPS)
-
-    def m_first(h, step, g):
-        return remote(
-            m_ref.at[h, pl.ds(GROUP * g, GROUP)], m_slot(ctx, g), m_send, m_recv.at[2 * ctx + g],
-            (2 * m_near(step) + h, head),
-        )
-
-    def m_sibling(g):
-        return remote(
-            m_ref.at[1 - core, pl.ds(GROUP * g, GROUP)], m_slot(ctx, g), m_send, m_recv.at[2 * ctx + g],
-            (sibling, head),
-        )
-
-    def m_next(source, g, step):
-        return remote(
-            m_slot(source, g), m_slot(source, g), m_send, m_recv.at[2 * source + g],
-            (2 * m_near(step) + core, head),
-        )
-
-    def forward(k, g):
-        for step in (1, -1):
-            for s in range(2):
-                last = 4 if (s == 0) == (step == 1) else 3
-                if k > last:
-                    continue
-                source = 2 * m_near(-step * k) + s
-                m_next(source, g, step).wait_recv()
-                if k < last:
-                    m_next(source, g, step).start()
+    def at(h, p, c):
+        return 2 * lax.rem(CHIPS // 2 * h + p, CHIPS) + c
+
+    def m_leave(h, g):
+        p = lax.rem(chip + CHIPS - CHIPS // 2 * h, CHIPS)
+        mine = m_ref.at[h, pl.ds(GROUP * g, GROUP)]
+
+        @pl.when(p < 2)
+        def _():
+            remote(mine, m_slot(ctx, g), m_send, m_recv.at[2 * p + g], (at(h, 1 - p, core), head)).start()
+            remote(mine, m_slot(ctx, g), m_send, m_pass, (sibling, head)).start()
+
+        @pl.when(p >= 2)
+        def _():
+            to = at(h, lax.div(CHIPS - 1 - p, 3), core)
+            remote(mine, m_slot(ctx, g), m_send, m_recv.at[2 * p + g], (to, head)).start()
+
+    def m_share(side, d, g, onward):
+        p = lax.rem(side + (2 * side - 1) * d + CHIPS, CHIPS)
+        slot = m_slot(at(root_head, p, core), g)
+        copy = remote(slot, slot, m_send, m_recv.at[2 * p + g], (at(root_head, 1 - root_chip, core), head))
+        copy.wait_recv()
+        if onward:
+            copy.start()
+        remote(slot, slot, m_send, m_pass, (sibling, head)).start()
+
+    def near(d, g):
+        m_share(root_chip, d, g, True)
+
+    def far(d, g):
+        m_share(1 - root_chip, d, g, False)
 
     def attend_locally(chains):
         for c in chains:
@@ -252,16 +259,15 @@
             shift = mm(c["kt2"], jnp.concatenate([high, low], axis=0))
             i, h = c["i"], c["h"]
             m_ref[h, i] = shift[:, DV:].T.astype(BF16)
-            o_ref[h, :, i] = shift[:, :DV].T.reshape(CHIPS, SLICE, DK).astype(BF16)
+            o_ref[h, :, i] = shift[:, :DV].T.reshape(ROOTS, SLICE, DK).astype(BF16)
             decay = c["decay"].astype(BF16).astype(F32)
             d_ref[h, i : i + 1, :] = decay
             d_ref[h, 8 + i : 9 + i, :] = c["decay"] - decay
         everything += chains
         if g == 0:
             pl.semaphore_wait(barrier, PEERS - 1 + 2 * (SIDE - 1))
-        for h, step in ((0, 1), (0, -1), (1, 1), (1, -1)):
-            m_first(h, step, g).start()
-        m_sibling(g).start()
+        for h in range(HEADS):
+            m_leave(h, g)
         if g == 0:
             for k in range(1, SIDE):
                 w_copy(k).start()
@@ -272,18 +278,33 @@
             for copy in w_own:
                 copy.start()
 
-    forward(1, 0)
+    @pl.when(is_root)
+    def _():
+        near(1, 0)
+        far(0, 0)
+        near(2, 0)
+
     for h in range(HEADS):
-        o_ref[h, :, LOCAL] = jnp.broadcast_to(d_ref[h].astype(BF16), (CHIPS, SLICE, DK))
-    for k in range(1, PEERS):
-        o_copy(k).start()
-    m_all[pl.ds(LOCAL * ctx, LOCAL)] = m_ref[core]
-    o_all[ctx] = o_ref[core, chip]
-    forward(1, 1)
+        o_ref[h, :, LOCAL] = jnp.broadcast_to(d_ref[h].astype(BF16), (ROOTS, SLICE, DK))
+        for r in range(ROOTS):
+
+            @pl.when(ctx != PEERS // 2 * h + r)
+            def _():
+                o_copy(h, r).start()
+
     attend_locally(everything[: len(everything) // 2])
-    forward(2, 0)
+
+    @pl.when(is_root)
+    def _():
+        m_all[pl.ds(LOCAL * ctx, LOCAL)] = m_ref[root_head]
+        o_all[ctx] = o_ref[root_head, column]
+        far(1, 0)
+        near(3, 0)
+        far(2, 0)
+        near(1, 1)
+        far(3, 0)
+
     attend_locally(everything[len(everything) // 2 :])
-    forward(2, 1)
 
     lanes = lax.broadcasted_iota(jnp.int32, (1, SPAN), 1)
     found = jnp.zeros((1, SPAN), jnp.int32)
@@ -298,49 +319,50 @@
         bits = bits | (jnp.int32(1) << start)
         start = start + prompt_ref[i]
 
-    for k in (3, 4):
-        for g in range(LOCAL // GROUP):
-            forward(k, g)
-    for g in range(LOCAL // GROUP):
-        m_next(sibling, g, 0).wait_recv()
-    finish_arrivals(o_all.at[pl.ds(0, PEERS - 1)], o_recv)
-    for source in range(PEERS):
-        tile = o_all[source, LOCAL].astype(F32)
-        d_all[source * 8 : source * 8 + 8, :] = tile[:8] + tile[8:]
+    def chains_here():
+        far(0, 1)
+        near(2, 1)
+        far(1, 1)
+        near(3, 1)
+        far(2, 1)
+        far(3, 1)
+        finish_arrivals(m_all.at[pl.ds(0, LOCAL * CHIPS)], m_pass)
+        finish_arrivals(o_all.at[pl.ds(0, PEERS - 1)], o_recv)
+        for source in range(PEERS):
+            tile = o_all[source, LOCAL, :16].astype(F32)
+            d_all[source * 8 : source * 8 + 8, :] = tile[:8] + tile[8:]
+        def advance(state, t):
+            slot = arr_ref[t]
+            stream[t] = state.astype(BF16)
+            high, low = split(state)
+            moved = mm(jnp.concatenate([high, low], axis=0), m_all[slot])
+            source, i = lax.div(slot, LOCAL), lax.rem(slot, LOCAL)
+            decay = d_all[pl.ds(source * 8 + i, 1), :]
+            return decay * state + o_all[source, i].astype(F32) - (moved[:SLICE] + moved[SLICE:])
+
+        def step(t, pair):
+            keep = (1 - ((bits >> t) & 1)).astype(F32)
+            return advance(keep * pair[0], t), advance(pair[1], t + CHAIN)
+
+        empty = jnp.zeros((SLICE, DK), F32)
+        lax.fori_loop(0, CHAIN, step, (empty, empty), unroll=16)
+
+        def place(a, carry):
+            states[a] = stream[inv_ref[0, a]]
+            return carry
+
+        lax.fori_loop(0, BLOCKS, place, 0, unroll=8)
+
+        mine = entry.at[root_head, :, pl.ds(pl.multiple_of(SLICE * column, SLICE), SLICE), :]
+        for k in range(1, PEERS):
+            to = ctx_peer(k)
+            remote(
+                states.at[pl.ds(LOCAL * to, LOCAL)], mine, s_send, s_recv.at[root_head], (to, head)
+            ).start()
+        mine[...] = states[pl.ds(LOCAL * ctx, LOCAL)]
+
     inv_copy.wait()
-
-    def advance(state, t):
-        slot = arr_ref[t]
-        stream[t] = state.astype(BF16)
-        high, low = split(state)
-        moved = mm(jnp.concatenate([high, low], axis=0), m_all[slot])
-        source, i = lax.div(slot, LOCAL), lax.rem(slot, LOCAL)
-        decay = d_all[pl.ds(source * 8 + i, 1), :]
-        return decay * state + o_all[source, i].astype(F32) - (moved[:SLICE] + moved[SLICE:])
-
-    def step(t, pair):
-        keep = (1 - ((bits >> t) & 1)).astype(F32)
-        return advance(keep * pair[0], t), advance(pair[1], t + CHAIN)
-
-    empty = jnp.zeros((SLICE, DK), F32)
-    lax.fori_loop(0, CHAIN, step, (empty, empty), unroll=16)
-
-    def place(a, carry):
-        states[a] = stream[inv_ref[0, a]]
-        return carry
-
-    lax.fori_loop(0, BLOCKS, place, 0, unroll=8)
-
-    def s_rows(h, z):
-        return entry.at[h, :, pl.ds(pl.multiple_of(SLICE * z, SLICE), SLICE), :]
-
-    def s_copy(k):
-        to = ctx_peer(k)
-        return remote(states.at[pl.ds(LOCAL * to, LOCAL)], s_rows(core, chip), s_send, s_recv, (to, head))
-
-    for k in range(1, PEERS):
-        s_copy(k).start()
-    entry[core, :, pl.ds(pl.multiple_of(SLICE * chip, SLICE), SLICE), :] = states[pl.ds(LOCAL * ctx, LOCAL)]
+    pl.when(is_root)(chains_here)
     for copy in w_own:
         copy.wait()
     finish_arrivals(w_all.at[0, pl.ds(0, SIDE - 1)], w_recv)
@@ -348,7 +370,15 @@
         w_pass(k).start()
     for load in loads[5:]:
         load.wait()
-    finish_arrivals(states.at[pl.ds(0, LOCAL * (PEERS - 1))], s_recv)
+    for h in range(HEADS):
+
+        @pl.when(root_of(h))
+        def _():
+            finish_arrivals(states.at[pl.ds(0, LOCAL * (ROOTS - 1))], s_recv.at[h])
+
+        @pl.when(jnp.logical_not(root_of(h)))
+        def _():
+            finish_arrivals(states.at[pl.ds(0, LOCAL * ROOTS)], s_recv.at[h])
 
     def n_copy(k):
         return remote(
@@ -410,9 +440,17 @@
         for k in range(1, SIDE):
             total = total + got[piece, k].astype(F32)
         out_ref[:, piece * PIECE : (piece + 1) * PIECE] = total.astype(BF16)
-    finish_sends(m_all.at[pl.ds(0, LOCAL * (PEERS - 1))], m_send)
-    finish_sends(o_all.at[pl.ds(0, PEERS - 1)], o_send)
-    finish_sends(states.at[pl.ds(0, LOCAL * (PEERS - 1))], s_send)
+    @pl.when(is_root)
+    def _():
+        finish_sends(m_all.at[pl.ds(0, 26 * GROUP)], m_send)
+        finish_sends(o_all.at[pl.ds(0, HEADS * ROOTS - 1)], o_send)
+        finish_sends(states.at[pl.ds(0, LOCAL * (PEERS - 1))], s_send)
+
+    @pl.when(jnp.logical_not(is_root))
+    def _():
+        finish_sends(m_all.at[pl.ds(0, 4 * GROUP)], m_send)
+        finish_sends(o_all.at[pl.ds(0, HEADS * ROOTS)], o_send)
+
     finish_sends(w_all.at[0, pl.ds(0, SIDE - 1)], w_send)
     finish_sends(w_all.at[0, pl.ds(0, SIDE - 1)], c_send)
     finish_sends(rows_all.at[0, pl.ds(0, SIDE - 1)], n_send)
@@ -440,7 +478,7 @@
             pltpu.VMEM((HEADS, tokens), BF16),
             pltpu.VMEM((1, DV), F32),
             pltpu.VMEM((HEADS, LOCAL, DK, DK), BF16),
-            pltpu.VMEM((HEADS, CHIPS, LOCAL + 1, SLICE, DK), BF16),
+            pltpu.VMEM((HEADS, ROOTS, LOCAL + 1, SLICE, DK), BF16),
             pltpu.VMEM((HEADS, SLICE, DK), F32),
             pltpu.VMEM((HEADS, LOCAL, SPAN, DK), F32),
             pltpu.VMEM((HEADS, LOCAL, SPAN, DV), F32),
@@ -458,8 +496,8 @@
             pltpu.VMEM((PIECES, SIDE, 32, PIECE), BF16),
             pltpu.VMEM((PIECES, SIDE, 32, PIECE), BF16),
             dma((7,)), dma, dma, dma, dma((2,)), dma, dma,
-            dma, dma((2 * PEERS,)), dma, dma,
-            dma, dma, dma, dma, dma, dma, dma, dma((PIECES,)),
+            dma, dma((2 * CHIPS,)), dma, dma, dma,
+            dma, dma((HEADS,)), dma, dma, dma, dma, dma, dma((PIECES,)),
         ],
         compiler_params=pltpu.CompilerParams(
             collective_id=0, has_side_effects=True, vmem_limit_bytes=VMEM_LIMIT

time: 67.1 us -> 70.1 us (1.045)
  Pallas kernels: 66.3 us -> 69.3 us
    pallas_call x1, Pallas kernels: 66.3 us -> 69.3 us  [per_device(): pl.pallas_call(main_kernel, out_shape=pltpu.VMEM((tokens // PEERS, MODEL)...]
where the time goes in v4:
time: 70.1 us; the launch traced here: 70 us
  Pallas kernels  69.3 us (99%)
    pallas_call x1, Pallas kernels, per_device(): pl.pallas_call(main_kernel, out_shape=pltpu.VMEM((tokens // PEERS, MODEL)...  69.3 us

profile of v4, /device:TPU:1, one launch (start us, length us, event | category | flops | bytes accessed | tf_op | source)
XLA Modules:
  0.0 70.0 jit_solution(8467277012701760347)
XLA Ops:
  0.0 69.3 %shard_map.100 = bf16[32,2048]{1,0:T(8,128)(2,1)S(1)} custom-call(s32[64]{0:T(128)} %arr_ref.1, s32[8]{0:T(128)} %prompt_ref.1, bf16[512,128]{1,0:T(8,128)(2,1)} %q_hbm.1, bf16[512,128]{1,0:T(8,128)(2,1)} %k_hbm.1, bf16[512,256]{1,0:T(8,128)(2,1)} %v_hbm.1, bf16[512,256]{1,0:T(8,128)(2,1)} %gate_hbm.1, bf16[2,512]{1,0:T(2,128)(2,1)} %bitcast.3, ...), custom_call_target="tpu_custom_call" | custom-call | tf_op jit(solution)/shard_map/pallas_call | solution.py:467
  69.3 0.7 copy.12

commit v5 on v3

--- a/solution.py
+++ b/solution.py
@@ -85,7 +85,7 @@
     out_ref,
     q_ref, k_ref, v_ref, gate_ref, beta_ref, decay_ref, gain_ref,
     m_ref, o_ref, d_ref, ql_ref, lo_ref, inv_vmem, inv_ref,
-    m_all, o_all, d_all, stream, states, entry, normed, rows_all, w_all, part, got,
+    m_all, o_all, d_all, stream, states, entry, gated, normed, rows_all, w_all, part, got,
     in_sem, inv_sem, w_send, w_recv, w_local, c_send, c_recv, m_send, m_recv, o_send, o_recv,
     s_send, s_recv, n_send, n_recv, r_send, r_recv, p_send, p_recv,
 ):
@@ -262,15 +262,6 @@
         for h, step in ((0, 1), (0, -1), (1, 1), (1, -1)):
             m_first(h, step, g).start()
         m_sibling(g).start()
-        if g == 0:
-            for k in range(1, SIDE):
-                w_copy(k).start()
-            w_own = [
-                pltpu.make_async_copy(w_half(half), w_all.at[half, side], w_local.at[half])
-                for half, side in enumerate((side_y, side_x))
-            ]
-            for copy in w_own:
-                copy.start()
 
     forward(1, 0)
     for h in range(HEADS):
@@ -298,9 +289,18 @@
         bits = bits | (jnp.int32(1) << start)
         start = start + prompt_ref[i]
 
-    for k in (3, 4):
-        for g in range(LOCAL // GROUP):
-            forward(k, g)
+    forward(3, 0)
+    forward(3, 1)
+    for k in range(1, SIDE):
+        w_copy(k).start()
+    w_own = [
+        pltpu.make_async_copy(w_half(half), w_all.at[half, side], w_local.at[half])
+        for half, side in enumerate((side_y, side_x))
+    ]
+    for copy in w_own:
+        copy.start()
+    forward(4, 0)
+    forward(4, 1)
     for g in range(LOCAL // GROUP):
         m_next(sibling, g, 0).wait_recv()
     finish_arrivals(o_all.at[pl.ds(0, PEERS - 1)], o_recv)
@@ -341,13 +341,17 @@
     for k in range(1, PEERS):
         s_copy(k).start()
     entry[core, :, pl.ds(pl.multiple_of(SLICE * chip, SLICE), SLICE), :] = states[pl.ds(LOCAL * ctx, LOCAL)]
+    for load in loads[5:]:
+        load.wait()
+    gain = jnp.concatenate([gain_ref[...]] * HEADS, axis=1)
+    for i in range(LOCAL):
+        gate = gate_ref[i * SPAN : (i + 1) * SPAN, :].astype(F32)
+        gated[i] = gain * (gate / (1.0 + jnp.exp(-gate)))
     for copy in w_own:
         copy.wait()
     finish_arrivals(w_all.at[0, pl.ds(0, SIDE - 1)], w_recv)
     for k in range(1, SIDE):
         w_pass(k).start()
-    for load in loads[5:]:
-        load.wait()
     finish_arrivals(states.at[pl.ds(0, LOCAL * (PEERS - 1))], s_recv)
 
     def n_copy(k):
@@ -358,7 +362,6 @@
     def r_copy(i):
         return remote(normed.at[i], rows_all.at[1, side_x], r_send, r_recv, (ctx, i * SIDE + side_y))
 
-    gain = gain_ref[...]
     for i in range(LOCAL):
         for h in range(HEADS):
             high, low = split(ql_ref[h, i])
@@ -366,8 +369,7 @@
             both = mm_t(jnp.concatenate([high, low], axis=0), state)
             core_out = both[:SPAN] + both[SPAN:] + lo_ref[h, i]
             scale = lax.rsqrt(jnp.mean(core_out * core_out, axis=-1, keepdims=True) + 1e-6)
-            gate = gate_ref[i * SPAN : (i + 1) * SPAN, h * DV : (h + 1) * DV].astype(F32)
-            value = core_out * scale * gain * (gate / (1.0 + jnp.exp(-gate)))
+            value = core_out * scale * gated[i, :, h * DV : (h + 1) * DV]
             normed[i, :, :, h * DV : (h + 1) * DV] = value.astype(BF16).reshape(SIDE, 32, DV)
 
         @pl.when(i != side_x)
@@ -452,6 +454,7 @@
             pltpu.VMEM((BLOCKS, SLICE, DK), BF16),
             pltpu.VMEM((BLOCKS, SLICE, DK), BF16),
             pltpu.VMEM((HEADS, LOCAL, DV, DK), BF16),
+            pltpu.VMEM((LOCAL, SPAN, HEADS * DV), F32),
             pltpu.VMEM((LOCAL, SIDE, 32, HEADS * DV), BF16),
             pltpu.VMEM((2, SIDE, LOCAL, 32, HEADS * DV), BF16),
             pltpu.VMEM((2, SIDE, HEADS * DV, MODEL // 2), BF16),

time: 67.1 us -> 65.7 us (0.979)
  Pallas kernels: 66.3 us -> 65 us
    pallas_call x1, Pallas kernels: 66.3 us -> 65 us  [per_device(): pl.pallas_call(main_kernel, out_shape=pltpu.VMEM((tokens // PEERS, MODEL)...]
where the time goes in v5:
time: 65.7 us; the launch traced here: 65.6 us
  Pallas kernels  65 us (99%)
  local copies, waits for them, and re-layouts  0.66 us (1%)
    pallas_call x1, Pallas kernels, per_device(): pl.pallas_call(main_kernel, out_shape=pltpu.VMEM((tokens // PEERS, MODEL)...  65 us

profile of v5, /device:TPU:1, one launch (start us, length us, event | category | flops | bytes accessed | tf_op | source)
XLA Modules:
  0.0 65.6 jit_solution(18218679374865859049)
XLA Ops:
  0.0 65.0 %shard_map.100 = bf16[32,2048]{1,0:T(8,128)(2,1)S(1)} custom-call(s32[64]{0:T(128)} %arr_ref.1, s32[8]{0:T(128)} %prompt_ref.1, bf16[512,128]{1,0:T(8,128)(2,1)} %q_hbm.1, bf16[512,128]{1,0:T(8,128)(2,1)} %k_hbm.1, bf16[512,256]{1,0:T(8,128)(2,1)} %v_hbm.1, bf16[512,256]{1,0:T(8,128)(2,1)} %gate_hbm.1, bf16[2,512]{1,0:T(2,128)(2,1)} %bitcast.3, ...), custom_call_target="tpu_custom_call" | custom-call | tf_op jit(solution)/shard_map/pallas_call | solution.py:431
  65.0 0.7 %copy.12 = bf16[32,2048]{1,0:T(8,128)(2,1)} copy(bf16[32,2048]{1,0:T(8,128)(2,1)S(1)} %shard_map.100) | data formatting | bytes 262144

commit v6 on v5

--- a/solution.py
+++ b/solution.py
@@ -270,8 +270,8 @@
         o_copy(k).start()
     m_all[pl.ds(LOCAL * ctx, LOCAL)] = m_ref[core]
     o_all[ctx] = o_ref[core, chip]
+    attend_locally(everything[: len(everything) // 2])
     forward(1, 1)
-    attend_locally(everything[: len(everything) // 2])
     forward(2, 0)
     attend_locally(everything[len(everything) // 2 :])
     forward(2, 1)
@@ -325,11 +325,10 @@
     empty = jnp.zeros((SLICE, DK), F32)
     lax.fori_loop(0, CHAIN, step, (empty, empty), unroll=16)
 
-    def place(a, carry):
-        states[a] = stream[inv_ref[0, a]]
-        return carry
-
-    lax.fori_loop(0, BLOCKS, place, 0, unroll=8)
+    def place(to):
+        for i in range(LOCAL):
+            a = LOCAL * to + i
+            states[a] = stream[inv_ref[0, a]]
 
     def s_rows(h, z):
         return entry.at[h, :, pl.ds(pl.multiple_of(SLICE * z, SLICE), SLICE), :]
@@ -339,7 +338,9 @@
         return remote(states.at[pl.ds(LOCAL * to, LOCAL)], s_rows(core, chip), s_send, s_recv, (to, head))
 
     for k in range(1, PEERS):
+        place(ctx_peer(k))
         s_copy(k).start()
+    place(ctx)
     entry[core, :, pl.ds(pl.multiple_of(SLICE * chip, SLICE), SLICE), :] = states[pl.ds(LOCAL * ctx, LOCAL)]
     for load in loads[5:]:
         load.wait()
@@ -381,7 +382,6 @@
     rows_all[0, side_y] = normed[:, side_y]
     rows_all[1, side_x] = normed[side_x]
     finish_arrivals(w_all.at[0, pl.ds(0, SIDE - 1)], c_recv)
-    finish_arrivals(rows_all.at[0, pl.ds(0, SIDE - 1)], n_recv)
 
     def p_copy(piece, k):
         if piece < PIECES // 2:
@@ -393,11 +393,11 @@
             p_send, p_recv.at[piece], (ctx, to),
         )
 
-    for piece in range(PIECES):
+    order = list(range(PIECES // 2, PIECES)) + list(range(PIECES // 2))
+    for piece in order:
         half, off = divmod(piece * PIECE, MODEL // 2)
-        if piece == PIECES // 2:
-            finish_arrivals(rows_all.at[1, pl.ds(0, SIDE - 1)], r_recv)
         if off == 0:
+            finish_arrivals(rows_all.at[half, pl.ds(0, SIDE - 1)], r_recv if half else n_recv)
             left = jnp.concatenate(
                 [rows_all[half, n].reshape(SPAN, HEADS * DV) for n in range(SIDE)], axis=1
             )
@@ -406,7 +406,7 @@
         part[piece] = total.astype(BF16).reshape(SIDE, 32, PIECE)
         for k in range(1, SIDE):
             p_copy(piece, k).start()
-    for piece in range(PIECES):
+    for piece in order:
         total = part[piece, side_x if piece < PIECES // 2 else side_y].astype(F32)
         finish_arrivals(got.at[piece, pl.ds(1, SIDE - 1)], p_recv.at[piece])
         for k in range(1, SIDE):

time: 65.7 us -> 65.1 us (level)
  Pallas kernels: 65 us -> 64.3 us
where the time goes in v6:
time: 65.1 us; the launch traced here: 65 us
  Pallas kernels  64.3 us (99%)
  local copies, waits for them, and re-layouts  0.66 us (1%)
    pallas_call x1, Pallas kernels, per_device(): pl.pallas_call(main_kernel, out_shape=pltpu.VMEM((tokens // PEERS, MODEL)...  64.3 us

profile of v6, /device:TPU:1, one launch (start us, length us, event | category | flops | bytes accessed | tf_op | source)
XLA Modules:
  0.0 65.0 jit_solution(12452749286653380257)
XLA Ops:
  0.0 64.3 %shard_map.100 = bf16[32,2048]{1,0:T(8,128)(2,1)S(1)} custom-call(s32[64]{0:T(128)} %arr_ref.1, s32[8]{0:T(128)} %prompt_ref.1, bf16[512,128]{1,0:T(8,128)(2,1)} %q_hbm.1, bf16[512,128]{1,0:T(8,128)(2,1)} %k_hbm.1, bf16[512,256]{1,0:T(8,128)(2,1)} %v_hbm.1, bf16[512,256]{1,0:T(8,128)(2,1)} %gate_hbm.1, bf16[2,512]{1,0:T(2,128)(2,1)} %bitcast.3, ...), custom_call_target="tpu_custom_call" | custom-call | tf_op jit(solution)/shard_map/pallas_call | solution.py:431
  64.4 0.7 %copy.12 = bf16[32,2048]{1,0:T(8,128)(2,1)} copy(bf16[32,2048]{1,0:T(8,128)(2,1)S(1)} %shard_map.100) | data formatting | bytes 262144

commit v7 on v6

--- a/solution.py
+++ b/solution.py
@@ -323,7 +323,7 @@
         return advance(keep * pair[0], t), advance(pair[1], t + CHAIN)
 
     empty = jnp.zeros((SLICE, DK), F32)
-    lax.fori_loop(0, CHAIN, step, (empty, empty), unroll=16)
+    lax.fori_loop(0, CHAIN, step, (empty, empty), unroll=32)
 
     def place(to):
         for i in range(LOCAL):
@@ -355,9 +355,10 @@
         w_pass(k).start()
     finish_arrivals(states.at[pl.ds(0, LOCAL * (PEERS - 1))], s_recv)
 
-    def n_copy(k):
+    def n_copy(k, j):
+        pair = pl.ds(GROUP * j, GROUP)
         return remote(
-            normed.at[:, lax.rem(side_y + k, SIDE)], rows_all.at[0, side_y], n_send, n_recv, (ctx, y_peer(k))
+            normed.at[pair, lax.rem(side_y + k, SIDE)], rows_all.at[0, side_y, pair], n_send, n_recv, (ctx, y_peer(k))
         )
 
     def r_copy(i):
@@ -377,8 +378,10 @@
         def _():
             r_copy(i).start()
 
-    for k in range(1, SIDE):
-        n_copy(k).start()
+        if i % GROUP == GROUP - 1:
+            for k in range(1, SIDE):
+                n_copy(k, i // GROUP).start()
+
     rows_all[0, side_y] = normed[:, side_y]
     rows_all[1, side_x] = normed[side_x]
     finish_arrivals(w_all.at[0, pl.ds(0, SIDE - 1)], c_recv)

time: 65.1 us -> 65.1 us (level)
  no operation moved by 1% of the time
where the time goes in v7:
time: 65.1 us; the launch traced here: 65 us
  Pallas kernels  64.3 us (99%)
  local copies, waits for them, and re-layouts  0.66 us (1%)
    pallas_call x1, Pallas kernels, per_device(): pl.pallas_call(main_kernel, out_shape=pltpu.VMEM((tokens // PEERS, MODEL)...  64.3 us

profile of v7, /device:TPU:1, one launch (start us, length us, event | category | flops | bytes accessed | tf_op | source)
XLA Modules:
  0.0 65.0 jit_solution(4490773616279408100)
XLA Ops:
  0.0 64.3 %shard_map.100 = bf16[32,2048]{1,0:T(8,128)(2,1)S(1)} custom-call(s32[64]{0:T(128)} %arr_ref.1, s32[8]{0:T(128)} %prompt_ref.1, bf16[512,128]{1,0:T(8,128)(2,1)} %q_hbm.1, bf16[512,128]{1,0:T(8,128)(2,1)} %k_hbm.1, bf16[512,256]{1,0:T(8,128)(2,1)} %v_hbm.1, bf16[512,256]{1,0:T(8,128)(2,1)} %gate_hbm.1, bf16[2,512]{1,0:T(2,128)(2,1)} %bitcast.3, ...), custom_call_target="tpu_custom_call" | custom-call | tf_op jit(solution)/shard_map/pallas_call | solution.py:434
  64.3 0.7 %copy.12 = bf16[32,2048]{1,0:T(8,128)(2,1)} copy(bf16[32,2048]{1,0:T(8,128)(2,1)S(1)} %shard_map.100) | data formatting | bytes 262144
